TPU v7x, 512 devices: a whole 4x8x8 slice. The times are simulated.
512 devices in a mesh: rep: 8 (over y), shard: 64 (over x, z, core).
Axes of the slice: x: 4, y: 8, z: 8, core: 2. Of those that a mesh axis runs over, the one named last changes fastest.
Arguments:
- tokens_in: bfloat16 [8, 2048, 3072], P('rep', 'shard'), may hold values from -6 to 6
- grad_out: bfloat16 [8, 2048, 8192], P('rep', 'shard'), may hold values from -0.125 to 0.125
- error_old: float32 [8, 3072, 8192], P('rep', None, 'shard'), may hold values from -6 to 6
- q_prev: float32 [8192, 64], P('shard'), may hold values from -6 to 6
Outputs:
- approx: bfloat16 [3072, 8192], P(None, 'shard')
- new_error: float32 [8, 3072, 8192], P('rep', None, 'shard')
- q_new: float32 [8192, 64], P('shard')
All inputs are finite; a program needn't handle non-finite values.
Results may differ from a plain program's by a relative error of at most 0.0014.
Values may be sent and summed in bfloat16 or wider, within the bound.
No kernel may reach another device: no remote copies, remote signals or barrier semaphores. Data moves between devices by JAX's collectives and lax.ppermute only.
A program may use at most 64 MiB of HBM per device.

v0:
```python
import jax
import jax.numpy as jnp
from jax import lax
from jax.sharding import PartitionSpec as P


def orthogonal(left_rows, gram):
    lower = jnp.linalg.cholesky(gram)
    return lax.linalg.triangular_solve(
        lower, left_rows, left_side=False, lower=True, transpose_a=True
    )


def per_device(tokens_in, grad_out, error_old, q_prev):
    inputs = tokens_in[0]
    outgrad = grad_out[0]
    out_cols = lax.all_to_all(outgrad, "shard", split_axis=1, concat_axis=0, tiled=True)
    gathered = lax.all_gather(inputs, "shard", axis=0, tiled=True)
    grad = jnp.einsum("tr,tn->rn", gathered, out_cols, preferred_element_type=jnp.float32)
    merged = grad + error_old[0]
    partial_left = jnp.dot(merged, q_prev, precision=lax.Precision.HIGHEST)
    left = lax.psum(partial_left, ("rep", "shard"))
    gram = jnp.dot(left.T, left, precision=lax.Precision.HIGHEST)
    basis = orthogonal(left, gram)
    partial_right = jnp.dot(merged.T, basis, precision=lax.Precision.HIGHEST)
    q_new = lax.psum(partial_right, "rep") / lax.axis_size("rep")
    approx_full = jnp.dot(basis, q_new.T, precision=lax.Precision.HIGHEST)
    new_error = (merged - approx_full)[None]
    return (approx_full.astype(jnp.bfloat16), new_error, q_new)


def solution(mesh):
    placed = (
        P("rep", "shard", None),
        P("rep", "shard", None),
        P("rep", None, "shard"),
        P("shard", None),
    )
    return jax.shard_map(
        per_device,
        mesh=mesh,
        in_specs=placed,
        out_specs=(P(None, "shard"), P("rep", None, "shard"), P("shard", None)),
        check_vma=False,
    )
```

profile of v0, /device:TPU:1, one launch (start us, length us, event | category | flops | bytes accessed | tf_op | source)
XLA Modules:
  0.0 439.4 jit_solution(1146523231930497517)
XLA Ops:
  7.2 0.0 copy-start
  7.2 0.0 all-gather.3.cloned.1.call-start
  7.2 0.7 all-gather.3.cloned.1.call-update
  7.9 0.0 all-reduce.2.cloned.1.call-start
  8.0 1.2 copy.13
  9.1 0.3 copy.11
  9.5 33.0 %all_to_all.19 = bf16[32,64,128]{2,0,1:T(8,128)(2,1)S(1)} all-to-all(bf16[32,64,128]{2,0,1:T(8,128)(2,1)S(1)} %copy.11), channel_id=1, replica_groups=mesh['rep'=8,'shard'=64] {'shard'}, dimensions={1} | all-to-all | bytes 1048576 | tf_op jit(solution)/shard_map/all_to_all | solution.py:17
  42.5 70.9 %all-gather.3.cloned.1.call-done = bf16[1,2048,3072]{2,1,0:T(8,128)(2,1)} async-done(((bf16[1,32,3072]{2,1,0:T(8,128)(2,1)}), bf16[1,2048,3072]{2,1,0:T(8,128)(2,1)}) %all-gather.3.cloned.1.call-update) | async-done | bytes 12582928 | tf_op jit(solution)/shard_map/all_gather | solution.py:18
  113.4 7.1 %fusion.2 = f32[3072,128]{1,0:T(8,128)S(1)} fusion(bf16[2048,128]{1,0:T(8,128)(2,1)S(1)} %bitcast.34, bf16[1,2048,3072]{2,1,0:T(8,128)(2,1)} %all-gather.3.cloned.1.call-done, f32[1,3072,128]{2,1,0:T(8,128)} %param.6), kind=kOutput, calls=%fused_computation.2 | convolution fusion | flops 1611005952 | bytes 16252928 | tf_op jit(solution)/shard_map/tr,tn->rn/dot_general | solution.py:19
  120.4 2.7 fusion.9
  123.2 0.0 all-reduce.2.cloned.1.call-update
  123.2 267.7 %all-reduce.2.cloned.1.call-done = f32[3072,64]{0,1:T(8,128)} async-done(((f32[3072,64]{0,1:T(8,128)}), f32[3072,64]{0,1:T(8,128)}) %all-reduce.2.cloned.1.call-update) | async-done | bytes 786448 | tf_op jit(solution)/shard_map/psum | solution.py:22
  390.9 2.2 fusion.10
  393.1 0.1 copy.12
  393.2 5.8 %cholesky.16 = f32[64,64]{1,0:T(8,128)S(1)} custom-call(f32[64,64]{1,0:T(8,128)S(1)} %fusion.8), custom_call_target="Cholesky" | custom-call | tf_op jit(solution)/shard_map/jit(cholesky)/cholesky | solution.py:8
  399.1 0.6 compare_reduce_fusion
  399.8 0.7 fusion.5
  400.4 4.9 %custom-call.6 = f32[1,64,64]{1,2,0:T(8,128)S(1)} custom-call(f32[1,64,64]{2,1,0:T(8,128)S(1)} %fusion.5), custom_call_target="InvertDiagBlocksLowerTriangular" | custom-call | tf_op jit(solution)/shard_map/triangular_solve | solution.py:9
  405.3 0.0 copy-done.1
  405.3 0.8 fusion.6
  406.2 1.1 fusion.11
  407.3 21.2 %psum.15 = f32[128,64]{0,1:T(8,128)S(1)} all-reduce(f32[128,64]{0,1:T(8,128)S(1)} %fusion.11), channel_id=1, replica_groups=mesh['rep'=8,'shard'=64] {'rep'}, use_global_device_ids=true, to_apply=%region_3.4 | all-reduce | flops 8192 | bytes 65536 | tf_op jit(solution)/shard_map/psum | solution.py:26
  428.5 0.0 copy-start.2
  428.5 4.0 subtract_bitcast_fusion
  (6 shorter events, 0.1 us)
Async XLA Ops:
  7.2 113.3 %copy-start = (f32[128,64]{0,1:T(8,128)S(1)}, f32[128,64]{0,1:T(8,128)}, u32[]{:S(2)}) copy-start(f32[128,64]{0,1:T(8,128)} %param.7) | copy-start | bytes 98308
  7.2 106.2 %all-gather.3.cloned.1.call-start = ((), (), s32[]{:S(2)}) async-start(), calls=%async_computation.2 | async-start | bytes 12779520 | tf_op jit(solution)/shard_map/all_gather | solution.py:18
  7.9 383.0 %all-reduce.2.cloned.1.call-start = ((), (), s32[]{:S(2)}) async-start(), calls=%async_computation.1 | async-start | bytes 1572864 | tf_op jit(solution)/shard_map/psum | solution.py:22
  390.9 14.4 %copy-start.1 = (f32[3072,64]{0,1:T(8,128)S(1)}, f32[3072,64]{0,1:T(8,128)}, u32[]{:S(2)}) copy-start(f32[3072,64]{0,1:T(8,128)} %all-reduce.2.cloned.1.call-done) | copy-start | bytes 2359300
  428.5 4.0 copy-start.2
Sparse Core Ops, SparseCore 0:
  11.3 101.9 all-gather.2
  123.3 267.5 all-reduce.1
where the time goes:
time: 446 us; the launch traced here: 439 us
  waiting for transfers between devices  339 us (76%)
  blocking collectives  54.2 us (12%)
  matrix products  17.9 us (4%)
  between operations  14.1 us (3%)
  other arithmetic  12.1 us (3%)
    psum x1, waiting for transfers between devices, per_device(): left = lax.psum(partial_left, ('rep', 'shard'))  268 us
    all_gather x1, waiting for transfers between devices, per_device(): gathered = lax.all_gather(inputs, 'shard', axis=0, tiled=True)  70.9 us
    all_to_all x1, blocking collectives, per_device(): lax.all_to_all(outgrad, 'shard', split_axis=1, concat_axis=0, tiled=True)  33 us
    psum x1, blocking collectives, per_device(): q_new = lax.psum(partial_right, 'rep') / lax.axis_size('rep')  21.2 us
  transfers between devices with their start and end apart: 2, of which 2 were waited for; matrix products, arithmetic and copies ran while one was open for 0% of the time, Pallas kernels for 0%

commit v1 on v0

v1 whole, which is shorter than its diff:
```python
import jax
import jax.numpy as jnp
from jax import lax
from jax.experimental import pallas as pl
from jax.experimental.pallas import tpu as pltpu
from jax.sharding import Mesh, PartitionSpec as P

F32 = jnp.float32
BF16 = jnp.bfloat16
HIGHEST = lax.Precision.HIGHEST
GROUP = ("x", "z")
PEERS = ("rep", "x", "core")
SWAP = [(0, 1), (1, 0)]
LANES = 128


def split(value):
    high = value.astype(BF16)
    return high, (value - high.astype(F32)).astype(BF16)


def dot_nt(a, b, precision=None):
    return lax.dot_general(a, b, (((1,), (1,)), ((), ())), precision=precision, preferred_element_type=F32)


def dot_nn(a, b, precision=None):
    return lax.dot_general(a, b, (((1,), (0,)), ((), ())), precision=precision, preferred_element_type=F32)


def dot_tn(a, b, precision=None):
    return lax.dot_general(a, b, (((0,), (0,)), ((), ())), precision=precision, preferred_element_type=F32)


def shaped(*shape, dtype=F32):
    return jax.ShapeDtypeStruct(shape, dtype)


def size_of(value):
    count = value.dtype.itemsize
    for extent in value.shape:
        count *= extent
    return count


def cost(flops, values):
    return pl.CostEstimate(flops=flops, bytes_accessed=sum(size_of(v) for v in values), transcendentals=0)


def vmem_call(body, out_shape, *args, flops=0, scratch=()):
    whole = pl.BlockSpec(memory_space=pltpu.VMEM)
    many = isinstance(out_shape, (tuple, list))
    return pl.pallas_call(
        body,
        out_shape=out_shape,
        in_specs=[whole] * len(args),
        out_specs=tuple(whole for _ in out_shape) if many else whole,
        scratch_shapes=scratch,
        cost_estimate=cost(flops, list(args) + (list(out_shape) if many else [out_shape])),
        compiler_params=pltpu.CompilerParams(vmem_limit_bytes=32 << 20),
    )(*args)


def steps_of(rows, step=512):
    step = min(rows, step)
    return [(start, step) for start in range(0, rows, step)]


def error_parts(q_ref, e_ref, left_ref, turned_ref):
    rank = q_ref.shape[0]
    q_high, q_low = split(q_ref[...])
    both = jnp.concatenate([q_high, q_low], axis=0)
    for start, step in steps_of(e_ref.shape[0]):
        cols = pl.ds(start, step)
        turned = e_ref[cols, :].T
        turned_ref[:, cols] = turned
        e_high, e_low = split(turned)
        wide = dot_nn(both, e_high)
        left_ref[:, cols] = wide[:rank] + (wide[rank:] + dot_nn(q_high, e_low))


def project(q_ref, q2_ref, cols_ref, out_ref, keep_ref, send_ref):
    rank = q_ref.shape[0]
    peers, _, count, _ = cols_ref.shape
    parts = []
    for ref in (q_ref, q2_ref):
        high, low = split(ref[...])
        parts.append(jnp.concatenate([high, low], axis=0))
    half = count // 2
    lane = lax.broadcasted_iota(jnp.int32, (half, LANES), 1)
    group = max(1, 128 // count)
    for j in range(0, peers, group):
        keep = cols_ref[j : j + group, 0].reshape(group * count, LANES)
        send = cols_ref[j : j + group, 1].reshape(group * count, LANES)
        wide = dot_nt(keep, parts[0]) + dot_nt(send, parts[1])
        value = wide + pltpu.roll(wide, rank, 1)
        for i in range(group):
            top = value[i * count : i * count + half]
            low = value[i * count + half : (i + 1) * count]
            out_ref[j + i] = jnp.where(lane < rank, top, low)
        cols = pl.ds(j * count, group * count)
        keep_ref[:, cols] = keep.astype(F32).T.astype(BF16)
        send_ref[:, cols] = send.astype(F32).T.astype(BF16)


def token_left(y_ref, tok_ref, add_ref, out_ref):
    rank = add_ref.shape[0]
    packed = jnp.sum(y_ref[...], axis=0)
    value = jnp.concatenate([packed, pltpu.roll(packed, rank, 1)], axis=0)
    high, low = split(value.T[:rank])
    both = jnp.concatenate([high, low], axis=0)
    bands = rank // 8
    blocks = out_ref.shape[0] // bands
    width = out_ref.shape[2]
    for c in range(blocks):
        cols = pl.ds(c * width, width)
        wide = dot_nn(both, tok_ref[:, cols])
        total = add_ref[:, cols] + (wide[:rank] + wide[rank:])
        for b in range(bands):
            out_ref[b * blocks + c] = total[b * 8 : (b + 1) * 8]


def unblock(left_ref, rank, c):
    bands = rank // 8
    blocks = left_ref.shape[0] // bands
    return jnp.concatenate([left_ref[b * blocks + c] for b in range(bands)], axis=0)


def left_forms(left_ref, wide_ref, tall_ref):
    rank = wide_ref.shape[0] // 2
    width = left_ref.shape[2]
    for c in range(wide_ref.shape[1] // width):
        high, low = split(unblock(left_ref, rank, c))
        both = jnp.concatenate([high, low], axis=0)
        cols = pl.ds(c * width, width)
        wide_ref[:, cols] = both
        tall_ref[cols, :] = both.astype(F32).T.astype(BF16)


def inverse_factor(left_ref, out_ref):
    rank = out_ref.shape[0]
    width = left_ref.shape[2]
    gram = jnp.zeros((rank, rank), F32)
    for c in range(left_ref.shape[0] // (rank // 8)):
        block = unblock(left_ref, rank, c)
        gram += dot_nt(block, block, HIGHEST)
    row_at = lax.broadcasted_iota(jnp.int32, (rank, rank), 0)
    col_at = lax.broadcasted_iota(jnp.int32, (rank, rank), 1)
    work = jnp.concatenate([gram, (row_at == col_at).astype(F32)], axis=1)
    tiles = [work[i * 8 : (i + 1) * 8] for i in range(rank // 8)]
    below = lax.broadcasted_iota(jnp.int32, (8, 1), 0)
    done = []
    for k in range(rank):
        at, sub = divmod(k, 8)
        row = tiles[at][sub : sub + 1, :]
        pivot = row[:, k : k + 1]
        scaled = row / pivot
        done.append(row * lax.rsqrt(pivot))
        for i in range(at, rank // 8):
            column = tiles[i][:, k : k + 1]
            if i == at:
                column = jnp.where(below > sub, column, 0.0)
            tiles[i] = tiles[i] - column * scaled
    out_ref[...] = jnp.concatenate(done, axis=0)[:, rank:]


def columns_product(cols_ref, tok_ref, out_ref):
    out_ref[...] = dot_nn(cols_ref[...], tok_ref[...])


def turned_grad(columns, gathered):
    own, tokens = columns.shape
    rows = gathered.shape[1]
    step = min(rows, 512)
    return pl.pallas_call(
        columns_product,
        out_shape=shaped(own, rows),
        grid=(rows // step,),
        in_specs=[
            pl.BlockSpec((own, tokens), lambda i: (0, 0)),
            pl.BlockSpec((tokens, step), lambda i: (0, i)),
        ],
        out_specs=pl.BlockSpec((own, step), lambda i: (0, i)),
        cost_estimate=cost(2 * own * tokens * rows, [columns, gathered]),
        compiler_params=pltpu.CompilerParams(vmem_limit_bytes=32 << 20),
    )(columns, gathered)


def merge(keep_ref, in_ref, e_ref, left_ref, merged_ref, right_ref):
    rank = left_ref.shape[0] // 2
    own, rows = keep_ref.shape
    top = jnp.zeros((2 * rank, own), F32)
    low = jnp.zeros((rank, own), F32)
    for start, step in steps_of(rows):
        cols = pl.ds(start, step)
        merged = (keep_ref[:, cols] + in_ref[:, cols]) + e_ref[:, cols]
        merged_ref[:, cols] = merged
        m_high, m_low = split(merged)
        top += dot_nt(left_ref[:, cols], m_high)
        low += dot_nt(left_ref[:rank, cols], m_low)
    right = top[:rank] + (top[rank:] + low)
    for g in range(right_ref.shape[0]):
        right_ref[g] = right


def turn(in_ref, out_ref):
    for start, step in steps_of(in_ref.shape[1]):
        out_ref[pl.ds(start, step), :] = in_ref[:, pl.ds(start, step)].T


def finish(right_ref, inverse_ref, left_ref, merged_ref, approx_ref, error_ref, q_ref):
    rank = inverse_ref.shape[0]
    reps = right_ref.shape[0]
    inverse = inverse_ref[...]
    right = jnp.sum(right_ref[...], axis=0)
    q_new = dot_nn(inverse, right, HIGHEST) / reps
    q_ref[...] = q_new
    high, low = split(dot_tn(inverse, q_new, HIGHEST))
    first = jnp.concatenate([high, high], axis=0)
    second = jnp.concatenate([low, jnp.zeros_like(low)], axis=0)
    left = left_ref[...]
    approx = dot_nn(left, first) + dot_nn(left, second)
    approx_ref[...] = approx.astype(BF16)
    error_ref[...] = merged_ref[...] - approx


def finished(right, inverse, left, merged):
    rows, own = merged.shape
    rank = inverse.shape[0]
    step = min(rows, 768)
    same = lambda i: (0, 0)
    block = lambda i: (i, 0)
    outs = (shaped(rows, own, dtype=BF16), shaped(rows, own), shaped(rank, own))
    return pl.pallas_call(
        finish,
        out_shape=outs,
        grid=(rows // step,),
        in_specs=[
            pl.BlockSpec(right.shape, lambda i: (0, 0, 0)),
            pl.BlockSpec(inverse.shape, same),
            pl.BlockSpec((step, 2 * rank), block),
            pl.BlockSpec((step, own), block),
        ],
        out_specs=(
            pl.BlockSpec((step, own), block),
            pl.BlockSpec((step, own), block),
            pl.BlockSpec((rank, own), same),
        ),
        cost_estimate=cost(6 * rows * rank * own, [right, left, merged] + list(outs)),
        compiler_params=pltpu.CompilerParams(vmem_limit_bytes=32 << 20),
    )(right, inverse, left, merged)


def direct(blocks, axes):
    return lax.all_to_all(blocks, axes, split_axis=0, concat_axis=0, tiled=True)


def spread(block, axes, count):
    return direct(jnp.broadcast_to(block[None], (count,) + block.shape), axes)


def per_device(sizes, tokens_in, grad_out, error_old, q_prev):
    tokens, outgrad, memory = tokens_in[0], grad_out[0], error_old[0]
    count, rows = tokens.shape
    own, rank = q_prev.shape
    members = sizes["x"] * sizes["z"]
    peers = sizes["rep"] * sizes["x"] * sizes["core"]
    core = lax.axis_index("core")

    gathered = lax.all_gather(tokens, GROUP, axis=0, tiled=True)
    q_t = q_prev.T
    q_t2 = lax.ppermute(q_t, "core", SWAP)
    cut = outgrad.reshape(count, members, 2, own).transpose(1, 2, 0, 3)
    cut = jnp.where(core == 0, cut, cut[:, ::-1])
    columns = direct(cut, GROUP)
    left_part, memory_t = vmem_call(
        error_parts, (shaped(rank, rows), shaped(own, rows)), q_t, memory, flops=6 * rank * rows * own
    )
    projected, keep, send = vmem_call(
        project,
        (
            shaped(members, count // 2, own),
            shaped(own, members * count, dtype=BF16),
            shaped(own, members * count, dtype=BF16),
        ),
        q_t,
        q_t2,
        columns,
        flops=8 * rank * own * members * count,
    )
    projected = direct(projected, GROUP)
    width = rows * rank // (8 * peers)
    left = vmem_call(token_left, shaped(peers, 8, width), projected, tokens, left_part, flops=4 * rank * count * rows)

    left = direct(left, PEERS).sum(0)
    left = spread(left, "z", sizes["z"]).sum(0)
    left = spread(left, PEERS, peers)

    left_wide, left_tall = vmem_call(
        left_forms, (shaped(2 * rank, rows, dtype=BF16), shaped(rows, 2 * rank, dtype=BF16)), left
    )
    inverse = vmem_call(inverse_factor, shaped(rank, rank), left, flops=12 * rank * rank * rows)

    grad_send = turned_grad(send, gathered)
    grad_in = lax.ppermute(grad_send, "core", SWAP)
    grad_keep = turned_grad(keep, gathered)
    merged_t, right = vmem_call(
        merge,
        (shaped(own, rows), shaped(sizes["rep"], rank, own)),
        grad_keep,
        grad_in,
        memory_t,
        left_wide,
        flops=6 * rank * own * rows,
    )
    right = direct(right, "rep")
    merged = vmem_call(turn, shaped(rows, own), merged_t)
    approx, new_error, q_new = finished(right, inverse, left_tall, merged)
    return approx, new_error[None], q_new.T


def solution(mesh):
    return build(mesh, (8, 4, 8, 2))


def build(mesh, shape):
    names = ("rep", "x", "z", "core")
    grid = Mesh(mesh.devices.reshape(shape), names)
    sizes = dict(zip(names, shape))
    shard = ("x", "z", "core")
    placed = (
        P("rep", shard, None),
        P("rep", shard, None),
        P("rep", None, shard),
        P(shard, None),
    )
    return jax.shard_map(
        lambda *args: per_device(sizes, *args),
        mesh=grid,
        in_specs=placed,
        out_specs=(P(None, shard), P("rep", None, shard), P(shard, None)),
        check_vma=False,
    )
```

time: 446 us -> 176 us (0.39); the launches traced: 439 us -> 175 us
  waiting for transfers between devices: 339 us -> 37 us
  starting transfers between devices: 0.08 us -> 39.9 us
  Pallas kernels: 0 us -> 20.6 us
  matrix products: 17.9 us -> 0 us
  local copies, waits for them, and re-layouts: 1.6 us -> 15 us
  other arithmetic: 12.1 us -> 1.04 us
  blocking collectives: 54.2 us -> 47.5 us
    psum x1 -> x0, waiting for transfers between devices: 268 us -> none  [per_device(): left = lax.psum(partial_left, ('rep', 'shard'))]
    all_gather x1, waiting for transfers between devices: 70.9 us -> 4.49 us  [per_device(): gathered = lax.all_gather(tokens, GROUP, axis=0, tiled=True)]
    all_to_all x0 -> x4, starting transfers between devices: none -> 33.8 us  [direct(): return lax.all_to_all(blocks, axes, split_axis=0, concat_axis=0, tiled=True)]
    all_to_all x0 -> x4, waiting for transfers between devices: none -> 31 us  [direct(): return lax.all_to_all(blocks, axes, split_axis=0, concat_axis=0, tiled=True)]
    psum x1 -> x0, blocking collectives: 21.2 us -> none  [per_device(): q_new = lax.psum(partial_right, 'rep') / lax.axis_size('rep')]
    pallas_call x0 -> x10, Pallas kernels: none -> 20.6 us  [the longest x7 11 us: vmem_call(): pl.pallas_call(body, out_shape=out_shape, in_specs=[whole] * len(args), o...]
    dot_general x5 -> x0, matrix products: 17.1 us -> none  [the longest x1 7.05 us: per_device(): jnp.einsum('tr,tn->rn', gathered, out_cols, preferred_element_type=jnp.fl...]
    all_to_all x1 -> x2, blocking collectives: 33 us -> 47.5 us  [direct(): return lax.all_to_all(blocks, axes, split_axis=0, concat_axis=0, tiled=True)]
  transfers between devices with their start and end apart: 2 -> 7, of which waited for: 2 -> 6; matrix products, arithmetic and copies ran while one was open for 0% -> 2% of each run, Pallas kernels for 0% -> 9%
where the time goes in v1:
time: 176 us; the launch traced here: 175 us
  blocking collectives  47.5 us (27%)
  starting transfers between devices  39.9 us (23%)
  waiting for transfers between devices  37 us (21%)
  Pallas kernels  20.6 us (12%)
  local copies, waits for them, and re-layouts  15 us (9%)
  between operations  14.2 us (8%)
    all_to_all x2, blocking collectives, direct(): return lax.all_to_all(blocks, axes, split_axis=0, concat_axis=0, tiled=True)  47.5 us
    all_to_all x4, starting transfers between devices, direct(): return lax.all_to_all(blocks, axes, split_axis=0, concat_axis=0, tiled=True)  33.8 us
    all_to_all x4, waiting for transfers between devices, direct(): return lax.all_to_all(blocks, axes, split_axis=0, concat_axis=0, tiled=True)  31 us
    unnamed x26, local copies, waits for them, and re-layouts  12 us
    pallas_call x7, Pallas kernels, vmem_call(): pl.pallas_call(body, out_shape=out_shape, in_specs=[whole] * len(args), o...  11 us
    pallas_call x2, Pallas kernels, turned_grad(): pl.pallas_call(columns_product, out_shape=shaped(own, rows), grid=(rows /...  6.15 us
    all_gather x1, waiting for transfers between devices, per_device(): gathered = lax.all_gather(tokens, GROUP, axis=0, tiled=True)  4.49 us
  transfers between devices with their start and end apart: 7, of which 6 were waited for; matrix products, arithmetic and copies ran while one was open for 2% of the time, Pallas kernels for 9%

profile of v1, /device:TPU:1, one launch (start us, length us, event | category | flops | bytes accessed | tf_op | source)
XLA Modules:
  0.0 175.2 jit_solution(16890681918512308982)
XLA Ops:
  7.9 1.4 reshape_squeeze.3
  10.9 13.7 %all-to-all-start = ((bf16[32,2,32,128]{3,2,1,0:T(8,128)(2,1)}), bf16[32,2,32,128]{3,2,1,0:T(8,128)(2,1)S(1)}, u32[]{:S(2)}, u32[]{:S(2)}) async-start(bf16[32,2,32,128]{3,2,1,0:T(8,128)(2,1)} %reverse_select_fusion), calls=%async_computation | async-start | bytes 1048576 | tf_op jit(solution)/shard_map/all_to_all | solution.py:254
  24.6 3.0 %collective-permute-start = (f32[64,128]{1,0:T(8,128)S(1)}, f32[64,128]{1,0:T(8,128)S(1)}, u32[]{:S(2)}, u32[]{:S(2)}) collective-permute-start(f32[64,128]{1,0:T(8,128)S(1)} %bitcast.13), channel_id=1, source_target_pairs={{0,1},{1,0},{2,3},{3,2},{4,5},{5,4},{6,7},{7,6},{8,9},{9,8},{10,11... | collective-permute-start | bytes 98312 | tf_op jit(solution)/shard_map/ppermute | solution.py:271
  28.5 10.4 %all-to-all-done.cols_ref = bf16[32,2,32,128]{3,2,1,0:T(8,128)(2,1)S(1)} async-done(((bf16[32,2,32,128]{3,2,1,0:T(8,128)(2,1)}), bf16[32,2,32,128]{3,2,1,0:T(8,128)(2,1)S(1)}, u32[]{:S(2)}, u32[]{:S(2)}) %all-to-all-start) | async-done | bytes 524320 | tf_op jit(solution)/shard_map/all_to_all | solution.py:254
  38.9 1.3 shard_map.67
  40.9 8.6 %all-to-all-start.1 = ((f32[32,16,128]{2,1,0:T(8,128)}), f32[32,16,128]{2,1,0:T(8,128)S(1)}, u32[]{:S(2)}, u32[]{:S(2)}) async-start(f32[32,16,128]{2,1,0:T(8,128)} %get-tuple-element.18), calls=%async_computation.1 | async-start | bytes 524288 | tf_op jit(solution)/shard_map/all_to_all | solution.py:254
  50.3 1.1 copy-done.3
  51.5 8.4 %all-to-all-done.1.y_ref = f32[32,16,128]{2,1,0:T(8,128)S(1)} async-done(((f32[32,16,128]{2,1,0:T(8,128)}), f32[32,16,128]{2,1,0:T(8,128)S(1)}, u32[]{:S(2)}, u32[]{:S(2)}) %all-to-all-start.1) | async-done | bytes 262176 | tf_op jit(solution)/shard_map/all_to_all | solution.py:254
  60.4 35.7 %all_to_all.30 = f32[64,8,384]{2,1,0:T(8,128)S(1)} all-to-all(f32[64,8,384]{2,1,0:T(8,128)S(1)} %shard_map.71), channel_id=1, replica_groups=mesh['rep'=8,'x'=4,'z'=8,'core'=2] {'rep','x','core'}, dimensions={0} | all-to-all | bytes 1572864 | tf_op jit(solution)/shard_map/all_to_all | solution.py:254
  96.2 11.8 %all_to_all.31 = f32[8,8,384]{2,1,0:T(8,128)S(1)} all-to-all(f32[8,8,384]{2,1,0:T(8,128)S(1)} %broadcast_in_dim.6), channel_id=1, replica_groups=mesh['rep'=8,'x'=4,'z'=8,'core'=2] {'z'}, dimensions={0} | all-to-all | bytes 196608 | tf_op jit(solution)/shard_map/all_to_all | solution.py:254
  108.9 7.5 %all-to-all-start.4 = ((f32[64,8,384]{2,1,0:T(8,128)}), f32[64,8,384]{2,1,0:T(8,128)S(1)}, u32[]{:S(2)}, u32[]{:S(2)}) async-start(f32[64,8,384]{2,1,0:T(8,128)} %broadcast_in_dim.7), calls=%async_computation.4 | async-start | bytes 1572864 | tf_op jit(solution)/shard_map/all_to_all | solution.py:254
  116.4 4.5 %all-gather.3.cloned.1.call-done = bf16[1,1024,3072]{2,1,0:T(8,128)(2,1)} async-done(((bf16[1,32,3072]{2,1,0:T(8,128)(2,1)}), bf16[1,1024,3072]{2,1,0:T(8,128)(2,1)}) %all-gather.3.cloned.1.call-update) | async-done | bytes 6291472 | tf_op jit(solution)/shard_map/all_gather | solution.py:269
  120.9 2.8 %copy-done = bf16[1,1024,3072]{2,1,0:T(8,128)(2,1)S(1)} copy-done((bf16[1,1024,3072]{2,1,0:T(8,128)(2,1)S(1)}, bf16[1,1024,3072]{2,1,0:T(8,128)(2,1)}, u32[]{:S(2)}) %copy-start) | copy-done | bytes 6291480
  123.7 3.7 %shard_map.69 = f32[128,3072]{1,0:T(8,128)} custom-call(bf16[128,1024]{1,0:T(8,128)(2,1)S(1)} %copy-done.11, bf16[1024,3072]{1,0:T(8,128)(2,1)S(1)} %bitcast.9), custom_call_target="tpu_custom_call" | custom-call | flops 805306368 | bytes 6553600 | tf_op jit(solution)/shard_map/pallas_call | solution.py:174
  127.4 3.1 %collective-permute-start.1 = (f32[128,3072]{1,0:T(8,128)}, f32[128,3072]{1,0:T(8,128)S(1)}, u32[]{:S(2)}, u32[]{:S(2)}) collective-permute-start(f32[128,3072]{1,0:T(8,128)} %shard_map.69), channel_id=1, source_target_pairs={{0,1},{1,0},{2,3},{3,2},{4,5},{5,4},{6,7},{7,6},{8,9},{9,8},{10,11... | collective-permute-start | bytes 4718600 | tf_op jit(solution)/shard_map/ppermute | solution.py:304
  130.5 8.7 %all-to-all-done.4.left_ref = f32[64,8,384]{2,1,0:T(8,128)S(1)} async-done(((f32[64,8,384]{2,1,0:T(8,128)}), f32[64,8,384]{2,1,0:T(8,128)S(1)}, u32[]{:S(2)}, u32[]{:S(2)}) %all-to-all-start.4) | async-done | bytes 786464 | tf_op jit(solution)/shard_map/all_to_all | solution.py:254
  140.4 2.8 %copy-done.1 = bf16[1,1024,3072]{2,1,0:T(8,128)(2,1)S(1)} copy-done((bf16[1,1024,3072]{2,1,0:T(8,128)(2,1)S(1)}, bf16[1,1024,3072]{2,1,0:T(8,128)(2,1)}, u32[]{:S(2)}) %copy-start.1) | copy-done | bytes 6291480
  143.2 2.5 %shard_map.68.keep_ref = f32[128,3072]{1,0:T(8,128)S(1)} custom-call(bf16[128,1024]{1,0:T(8,128)(2,1)S(1)} %get-tuple-element.15.cols_ref, bf16[1024,3072]{1,0:T(8,128)(2,1)S(1)} %bitcast.10), custom_call_target="tpu_custom_call" | custom-call | flops 805306368 | bytes 6553600 | tf_op jit(solution)/shard_map/pallas_call | solution.py:174
  146.8 1.4 copy-done.6
  148.2 1.4 shard_map.73
  149.6 4.0 %all-to-all-start.5 = ((f32[8,64,128]{2,1,0:T(8,128)}), f32[8,64,128]{2,1,0:T(8,128)S(1)}, u32[]{:S(2)}, u32[]{:S(2)}) async-start(f32[8,64,128]{2,1,0:T(8,128)} %get-tuple-element.21), calls=%async_computation.5 | async-start | bytes 524288 | tf_op jit(solution)/shard_map/all_to_all | solution.py:254
  153.6 6.3 %shard_map.74.inverse_ref = f32[64,64]{1,0:T(8,128)S(1)} custom-call(f32[64,8,384]{2,1,0:T(8,128)S(1)} %all-to-all-done.4.left_ref), custom_call_target="tpu_custom_call" | custom-call | flops 150994944 | bytes 802816 | tf_op jit(solution)/shard_map/pallas_call | solution.py:52
  160.4 3.4 %all-to-all-done.5.right_ref = f32[8,64,128]{2,1,0:T(8,128)S(1)} async-done(((f32[8,64,128]{2,1,0:T(8,128)}), f32[8,64,128]{2,1,0:T(8,128)S(1)}, u32[]{:S(2)}, u32[]{:S(2)}) %all-to-all-start.5) | async-done | bytes 262176 | tf_op jit(solution)/shard_map/all_to_all | solution.py:254
  164.9 3.4 %shard_map.76 = (bf16[3072,128]{1,0:T(8,128)(2,1)}, f32[3072,128]{1,0:T(8,128)}, f32[64,128]{1,0:T(8,128)}) custom-call(f32[8,64,128]{2,1,0:T(8,128)S(1)} %all-to-all-done.5.right_ref, f32[64,64]{1,0:T(8,128)S(1)} %shard_map.74.inverse_ref, bf16[3072,128]{1,0:T(8,128)(2,1)S(1)} %copy-done.8, f32[3072,128]{1,0:T(8,128)S(1)} %shard_map.75.merged_ref), custom_call_target="tpu_custom_call" | custom-call | flops 150994944 | bytes 5013504 | tf_op jit(solution)/shard_map/pallas_call | solution.py:233
  (36 shorter events, 10.0 us)
Async XLA Ops:
  7.2 113.8 %all-gather.3.cloned.1.call-start = ((), (), s32[]{:S(2)}) async-start(), calls=%async_computation.6 | async-start | bytes 6488064 | tf_op jit(solution)/shard_map/all_gather | solution.py:269
  9.3 15.3 %copy-start.12 = (f32[128,64]{0,1:T(8,128)S(1)}, f32[128,64]{0,1:T(8,128)}, u32[]{:S(2)}) copy-start(f32[128,64]{0,1:T(8,128)} %param.7) | copy-start | bytes 98308
  9.9 39.6 %copy-start.2 = (f32[1,3072,128]{2,1,0:T(8,128)S(1)}, f32[1,3072,128]{2,1,0:T(8,128)}, u32[]{:S(2)}) copy-start(f32[1,3072,128]{2,1,0:T(8,128)} %param.6) | copy-start | bytes 4718596
  10.9 28.0 %all-to-all-start = ((bf16[32,2,32,128]{3,2,1,0:T(8,128)(2,1)}), bf16[32,2,32,128]{3,2,1,0:T(8,128)(2,1)S(1)}, u32[]{:S(2)}, u32[]{:S(2)}) async-start(bf16[32,2,32,128]{3,2,1,0:T(8,128)(2,1)} %reverse_select_fusion), calls=%async_computation | async-start | bytes 1048576 | tf_op jit(solution)/shard_map/all_to_all | solution.py:254
  24.6 35.3 %copy-start.9 = (bf16[1,32,3072]{2,1,0:T(8,128)(2,1)S(1)}, bf16[1,32,3072]{2,1,0:T(8,128)(2,1)}, u32[]{:S(2)}) copy-start(bf16[1,32,3072]{2,1,0:T(8,128)(2,1)} %param.4) | copy-start | bytes 589828
  24.6 3.8 %collective-permute-start = (f32[64,128]{1,0:T(8,128)S(1)}, f32[64,128]{1,0:T(8,128)S(1)}, u32[]{:S(2)}, u32[]{:S(2)}) collective-permute-start(f32[64,128]{1,0:T(8,128)S(1)} %bitcast.13), channel_id=1, source_target_pairs={{0,1},{1,0},{2,3},{3,2},{4,5},{5,4},{6,7},{7,6},{8,9},{9,8},{10,11... | collective-permute-start | bytes 98312 | tf_op jit(solution)/shard_map/ppermute | solution.py:271
  40.2 0.7 copy-start.10
  40.9 19.0 %all-to-all-start.1 = ((f32[32,16,128]{2,1,0:T(8,128)}), f32[32,16,128]{2,1,0:T(8,128)S(1)}, u32[]{:S(2)}, u32[]{:S(2)}) async-start(f32[32,16,128]{2,1,0:T(8,128)} %get-tuple-element.18), calls=%async_computation.1 | async-start | bytes 524288 | tf_op jit(solution)/shard_map/all_to_all | solution.py:254
  50.3 1.2 copy-start.3
  96.2 24.7 %copy-start.11 = (bf16[128,1024]{1,0:T(8,128)(2,1)S(1)}, bf16[128,1024]{1,0:T(8,128)(2,1)}, u32[]{:S(2)}) copy-start(bf16[128,1024]{1,0:T(8,128)(2,1)} %copy-done.10) | copy-start | bytes 786436
  108.9 30.3 %all-to-all-start.4 = ((f32[64,8,384]{2,1,0:T(8,128)}), f32[64,8,384]{2,1,0:T(8,128)S(1)}, u32[]{:S(2)}, u32[]{:S(2)}) async-start(f32[64,8,384]{2,1,0:T(8,128)} %broadcast_in_dim.7), calls=%async_computation.4 | async-start | bytes 1572864 | tf_op jit(solution)/shard_map/all_to_all | solution.py:254
  120.9 2.8 %copy-start = (bf16[1,1024,3072]{2,1,0:T(8,128)(2,1)S(1)}, bf16[1,1024,3072]{2,1,0:T(8,128)(2,1)}, u32[]{:S(2)}) copy-start(bf16[1,1024,3072]{2,1,0:T(8,128)(2,1)} %all-gather.3.cloned.1.call-done) | copy-start | bytes 18874372
  127.4 18.3 %collective-permute-start.1 = (f32[128,3072]{1,0:T(8,128)}, f32[128,3072]{1,0:T(8,128)S(1)}, u32[]{:S(2)}, u32[]{:S(2)}) collective-permute-start(f32[128,3072]{1,0:T(8,128)} %shard_map.69), channel_id=1, source_target_pairs={{0,1},{1,0},{2,3},{3,2},{4,5},{5,4},{6,7},{7,6},{8,9},{9,8},{10,11... | collective-permute-start | bytes 4718600 | tf_op jit(solution)/shard_map/ppermute | solution.py:304
  139.5 0.9 copy-start.7
  140.4 2.8 %copy-start.1 = (bf16[1,1024,3072]{2,1,0:T(8,128)(2,1)S(1)}, bf16[1,1024,3072]{2,1,0:T(8,128)(2,1)}, u32[]{:S(2)}) copy-start(bf16[1,1024,3072]{2,1,0:T(8,128)(2,1)} %all-gather.3.cloned.1.call-done) | copy-start | bytes 18874372
  143.2 3.6 %copy-start.4 = (f32[128,3072]{1,0:T(8,128)S(1)}, f32[128,3072]{1,0:T(8,128)}, u32[]{:S(2)}) copy-start(f32[128,3072]{1,0:T(8,128)} %copy-done.3) | copy-start | bytes 4718596
  145.7 1.1 copy-start.5
  146.8 1.4 copy-start.6
  149.6 14.2 %all-to-all-start.5 = ((f32[8,64,128]{2,1,0:T(8,128)}), f32[8,64,128]{2,1,0:T(8,128)S(1)}, u32[]{:S(2)}, u32[]{:S(2)}) async-start(f32[8,64,128]{2,1,0:T(8,128)} %get-tuple-element.21), calls=%async_computation.5 | async-start | bytes 524288 | tf_op jit(solution)/shard_map/all_to_all | solution.py:254
  163.8 1.1 copy-start.8
Sparse Core Ops, SparseCore 0:
  11.2 109.7 all-gather.2

commit v2 on v1

v2 whole, which is shorter than its diff:
```python
import jax
import jax.numpy as jnp
from jax import lax
from jax.experimental import pallas as pl
from jax.experimental.pallas import tpu as pltpu
from jax.sharding import Mesh, PartitionSpec as P

F32 = jnp.float32
BF16 = jnp.bfloat16
HIGHEST = lax.Precision.HIGHEST
PEERS = ("rep", "x")
SWAP = [(0, 1), (1, 0)]
LANES = 128


def split(value):
    high = value.astype(BF16)
    return high, (value - high.astype(F32)).astype(BF16)


def dot_nt(a, b, precision=None):
    return lax.dot_general(a, b, (((1,), (1,)), ((), ())), precision=precision, preferred_element_type=F32)


def dot_nn(a, b, precision=None):
    return lax.dot_general(a, b, (((1,), (0,)), ((), ())), precision=precision, preferred_element_type=F32)


def dot_tn(a, b, precision=None):
    return lax.dot_general(a, b, (((0,), (0,)), ((), ())), precision=precision, preferred_element_type=F32)


def shaped(*shape, dtype=F32):
    return jax.ShapeDtypeStruct(shape, dtype)


def size_of(value):
    count = value.dtype.itemsize
    for extent in value.shape:
        count *= extent
    return count


def cost(flops, values):
    return pl.CostEstimate(flops=flops, bytes_accessed=sum(size_of(v) for v in values), transcendentals=0)


def vmem_call(body, out_shape, *args, flops=0, scratch=(), extra=0):
    whole = pl.BlockSpec(memory_space=pltpu.VMEM)
    many = isinstance(out_shape, (tuple, list))
    values = list(args) + (list(out_shape) if many else [out_shape])
    room = sum(size_of(v) for v in values) + extra
    return pl.pallas_call(
        body,
        out_shape=out_shape,
        in_specs=[whole] * len(args),
        out_specs=tuple(whole for _ in out_shape) if many else whole,
        scratch_shapes=scratch,
        cost_estimate=cost(flops, values),
        compiler_params=pltpu.CompilerParams(vmem_limit_bytes=room + (6 << 20)),
    )(*args)


def steps_of(rows, step=512):
    step = min(rows, step)
    return [(start, step) for start in range(0, rows, step)]


def error_parts(q_ref, e_ref, tok_ref, left_ref, turned_ref):
    rank = q_ref.shape[0]
    q_high, q_low = split(q_ref[...])
    both = jnp.concatenate([q_high, q_low], axis=0)
    for start, step in steps_of(e_ref.shape[0]):
        cols = pl.ds(start, step)
        turned = e_ref[cols, :].T
        turned_ref[:, cols] = turned
        e_high, e_low = split(turned)
        wide = dot_nn(both, e_high)
        left_ref[:rank, cols] = wide[:rank] + (wide[rank:] + dot_nn(q_high, e_low))
        left_ref[rank:, cols] = tok_ref[:, cols].astype(F32)


def cut_columns(in_ref, out_ref):
    deep, across, _, own = out_ref.shape
    for z in range(deep):
        for i in range(across):
            x, core = divmod(i, 2)
            start = ((x * deep + z) * 2 + core) * own
            out_ref[z, i] = in_ref[:, start : start + own]


def pack_factor(*refs):
    *q_refs, out_ref = refs
    across, rank = len(q_refs), q_refs[0].shape[1]
    x, core = lax.axis_index("x"), lax.axis_index("core")
    for shift, q_ref in enumerate(q_refs):
        source = lax.rem(x + across - shift, across)
        for i in (0, 1):
            high, low = split(q_ref[i])
            place = 2 * source + (core if i == 0 else 1 - core)
            out_ref[place] = jnp.concatenate([high, low], axis=0)


def project(q_ref, cols_ref, out_ref):
    near, wide, own = q_ref.shape
    rank = wide // 2
    deep, _, count, _ = cols_ref.shape
    total = jnp.zeros((deep * count, wide), F32)
    for i in range(near):
        total += dot_nt(cols_ref[:, i].reshape(deep * count, own), q_ref[i])
    value = total + pltpu.roll(total, rank, 1)
    half = count // 2
    lane = lax.broadcasted_iota(jnp.int32, (half, 2 * rank), 1)
    for z in range(deep):
        top = value[z * count : z * count + half]
        low = value[z * count + half : (z + 1) * count]
        packed = jnp.where(lane < rank, top, low)
        out_ref[2 * z] = packed
        out_ref[2 * z + 1] = packed


def pick_columns(cols_ref, *out_refs):
    across = len(out_refs)
    x = lax.axis_index("x")
    for shift, out_ref in enumerate(out_refs):
        out_ref[...] = cols_ref[:, pl.ds(2 * lax.rem(x + shift, across), 2)]


def turn_columns(*refs):
    *in_refs, out_ref = refs
    deep, _, count, own = in_refs[0].shape
    across = len(in_refs)
    x, core = lax.axis_index("x"), lax.axis_index("core")
    for shift, in_ref in enumerate(in_refs):
        source = lax.rem(x + across - shift, across)
        cols = pl.ds(pl.multiple_of(source * (deep * count), deep * count), deep * count)
        for i in (0, 1):
            block = in_ref[:, core if i == 0 else 1 - core].reshape(deep * count, own)
            out_ref[i * own : (i + 1) * own, cols] = block.astype(F32).T.astype(BF16)


def token_left(y_ref, add_ref, add2_ref, out_ref):
    rank, rows = y_ref.shape[2] // 2, add_ref.shape[1]
    core = lax.axis_index("core")
    packed = [y_ref[i] for i in (0, 1)]
    for z in range(1, y_ref.shape[0] // 2):
        packed = [packed[i] + y_ref[2 * z + i] for i in (0, 1)]
    ordered = [jnp.where(core == i, packed[0], packed[1]) for i in (0, 1)]
    value = jnp.concatenate(
        [part for one in ordered for part in (one, pltpu.roll(one, rank, 1))], axis=0
    )
    high, low = split(value.T[:rank])
    both = jnp.concatenate([high, low], axis=0)
    bands = rank // 8
    blocks = out_ref.shape[0] // bands
    width = out_ref.shape[2]
    for c in range(blocks):
        cols = pl.ds(pl.multiple_of(core * (rows // 2) + c * width, LANES), width)
        pair = jnp.concatenate([add_ref[rank:, cols], add2_ref[rank:, cols]], axis=0).astype(BF16)
        wide = dot_nn(both, pair)
        total = (add_ref[:rank, cols] + add2_ref[:rank, cols]) + (wide[:rank] + wide[rank:])
        for b in range(bands):
            out_ref[b * blocks + c] = total[b * 8 : (b + 1) * 8]


def add_spread(in_ref, out_ref):
    total = jnp.sum(in_ref[...], axis=0)
    for i in range(out_ref.shape[0]):
        out_ref[i] = total


def unblock(left_ref, rank, c):
    bands = rank // 8
    blocks = left_ref.shape[0] // bands
    return jnp.concatenate([left_ref[b * blocks + c] for b in range(bands)], axis=0)


def left_forms(mine_ref, other_ref, wide_ref, tall_ref):
    rank = wide_ref.shape[0] // 2
    rows = wide_ref.shape[1]
    width = mine_ref.shape[2]
    core = lax.axis_index("core")
    for ref, place in ((mine_ref, core), (other_ref, 1 - core)):
        for c in range(rows // 2 // width):
            high, low = split(unblock(ref, rank, c))
            both = jnp.concatenate([high, low], axis=0)
            cols = pl.ds(pl.multiple_of(place * (rows // 2) + c * width, LANES), width)
            wide_ref[:, cols] = both
            tall_ref[cols, :] = both.astype(F32).T.astype(BF16)


def inverse_factor(mine_ref, other_ref, out_ref):
    rank = out_ref.shape[0]
    grams = []
    for ref in (mine_ref, other_ref):
        gram = jnp.zeros((rank, rank), F32)
        for c in range(ref.shape[0] // (rank // 8)):
            block = unblock(ref, rank, c)
            gram += dot_nt(block, block, HIGHEST)
        grams.append(gram)
    gram = grams[0] + grams[1]
    row_at = lax.broadcasted_iota(jnp.int32, (rank, rank), 0)
    col_at = lax.broadcasted_iota(jnp.int32, (rank, rank), 1)
    work = jnp.concatenate([gram, (row_at == col_at).astype(F32)], axis=1)
    tiles = [work[i * 8 : (i + 1) * 8] for i in range(rank // 8)]
    below = lax.broadcasted_iota(jnp.int32, (8, 1), 0)
    done = []
    for k in range(rank):
        at, sub = divmod(k, 8)
        row = tiles[at][sub : sub + 1, :]
        pivot = row[:, k : k + 1]
        scaled = row / pivot
        done.append(row * lax.rsqrt(pivot))
        for i in range(at, rank // 8):
            column = tiles[i][:, k : k + 1]
            if i == at:
                column = jnp.where(below > sub, column, 0.0)
            tiles[i] = tiles[i] - column * scaled
    out_ref[...] = jnp.concatenate(done, axis=0)[:, rank:]


def turned_grad(cols_ref, e_ref, tok_ref, keep_ref, send_ref):
    own = keep_ref.shape[0]
    for start, step in steps_of(tok_ref.shape[1]):
        cols = pl.ds(start, step)
        both = dot_nn(cols_ref[...], tok_ref[:, cols])
        send_ref[:, cols] = both[own:]
        keep_ref[:, cols] = both[:own] + e_ref[:, cols]


def merge(keep_ref, in_ref, left_ref, merged_ref, right_ref):
    rank = left_ref.shape[0] // 2
    own, rows = keep_ref.shape
    top = jnp.zeros((2 * rank, own), F32)
    low = jnp.zeros((rank, own), F32)
    for start, step in steps_of(rows):
        cols = pl.ds(start, step)
        merged = keep_ref[:, cols] + in_ref[:, cols]
        merged_ref[:, cols] = merged
        m_high, m_low = split(merged)
        top += dot_nt(left_ref[:, cols], m_high)
        low += dot_nt(left_ref[:rank, cols], m_low)
    right = top[:rank] + (top[rank:] + low)
    for g in range(right_ref.shape[0]):
        right_ref[g] = right


def turn(in_ref, out_ref):
    for start, step in steps_of(in_ref.shape[1]):
        out_ref[pl.ds(start, step), :] = in_ref[:, pl.ds(start, step)].T


def finish(right_ref, inverse_ref, left_ref, merged_ref, approx_ref, error_ref, q_ref, weights):
    rank, own = q_ref.shape
    reps = right_ref.shape[0]

    @pl.when(pl.program_id(0) == 0)
    def _():
        inverse = inverse_ref[...]
        right = jnp.sum(right_ref[...], axis=0)
        q_new = dot_nn(inverse, right, HIGHEST) / reps
        q_ref[...] = q_new
        high, low = split(dot_tn(inverse, q_new, HIGHEST))
        weights[:rank, :own] = high
        weights[rank:, :own] = high
        weights[:rank, own:] = low
        weights[rank:, own:] = jnp.zeros_like(low)

    wide = dot_nn(left_ref[...], weights[...])
    approx = wide[:, :own] + wide[:, own:]
    approx_ref[...] = approx.astype(BF16)
    error_ref[...] = merged_ref[...] - approx


def finished(right, inverse, left, merged):
    rows, own = merged.shape
    rank = inverse.shape[0]
    step = min(rows, 768)
    same = lambda i: (0, 0)
    block = lambda i: (i, 0)
    outs = (shaped(rows, own, dtype=BF16), shaped(rows, own), shaped(rank, own))
    return pl.pallas_call(
        finish,
        out_shape=outs,
        grid=(rows // step,),
        in_specs=[
            pl.BlockSpec(right.shape, lambda i: (0, 0, 0)),
            pl.BlockSpec(inverse.shape, same),
            pl.BlockSpec((step, 2 * rank), block),
            pl.BlockSpec((step, own), block),
        ],
        out_specs=(
            pl.BlockSpec((step, own), block),
            pl.BlockSpec((step, own), block),
            pl.BlockSpec((rank, own), same),
        ),
        scratch_shapes=[pltpu.VMEM((2 * rank, 2 * own), BF16)],
        cost_estimate=cost(6 * rows * rank * own, [right, left, merged] + list(outs)),
        compiler_params=pltpu.CompilerParams(vmem_limit_bytes=60 << 20),
    )(right, inverse, left, merged)


def direct(blocks, axes):
    return lax.all_to_all(blocks, axes, split_axis=0, concat_axis=0, tiled=True)


def shifted(value, across, shift):
    return lax.ppermute(value, "x", [(i, (i + shift) % across) for i in range(across)])


def after(value, earlier):
    return lax.optimization_barrier((value, earlier))[0]


def per_device(sizes, tokens_in, grad_out, error_old, q_prev):
    tokens, outgrad, memory = tokens_in[0], grad_out[0], error_old[0]
    count, rows = tokens.shape
    own, rank = q_prev.shape
    reps, across, deep = sizes["rep"], sizes["x"], sizes["z"]
    peers = reps * across
    width = rows * rank // (16 * peers)

    gathered = lax.all_gather(tokens, ("x", "z"), axis=0, tiled=True)
    q_t = q_prev.T
    cut = vmem_call(cut_columns, shaped(deep, across * 2, count, own, dtype=BF16), outgrad)
    q_t, memory = lax.optimization_barrier((q_t, memory, cut))[:2]
    cut = direct(cut, "z")
    q_pair = jnp.stack([q_t, lax.ppermute(q_t, "core", SWAP)])
    q_near = [q_pair] + [shifted(q_pair, across, s) for s in range(1, across)]
    left_own, memory_t = vmem_call(
        error_parts,
        (shaped(rank + count, rows), shaped(own, rows)),
        q_t,
        memory,
        tokens,
        flops=6 * rank * rows * own,
    )
    q_near = vmem_call(pack_factor, shaped(2 * across, 2 * rank, own, dtype=BF16), *q_near)
    projected = vmem_call(
        project,
        shaped(deep * 2, count // 2, own),
        q_near,
        cut,
        flops=4 * rank * own * deep * across * 2 * count,
    )
    left_own2 = lax.ppermute(after(left_own, projected), "core", SWAP)
    projected = direct(projected, ("z", "core"))
    left = vmem_call(
        token_left,
        shaped(peers, 8, width),
        projected,
        left_own,
        left_own2,
        flops=4 * rank * count * rows,
    )
    late_cut = after(cut, left)
    chip = shaped(deep, 2, count, own, dtype=BF16)
    columns = vmem_call(pick_columns, (chip,) * across, late_cut)
    columns = [columns[0]] + [shifted(columns[s], across, s) for s in range(1, across)]
    columns = vmem_call(
        turn_columns,
        shaped(2 * own, deep * across * count, dtype=BF16),
        *columns,
    )
    left = direct(left, PEERS)
    left = vmem_call(add_spread, shaped(deep, 8, width), after(left, columns))
    left = direct(left, "z")
    summed = vmem_call(add_spread, shaped(peers, 8, width), left)
    left = direct(summed, PEERS)
    gathered = after(gathered, summed)
    grad_keep, grad_send = vmem_call(
        turned_grad,
        (shaped(own, rows), shaped(own, rows)),
        columns,
        memory_t,
        gathered,
        flops=4 * own * rows * deep * across * count,
    )
    grad_in = lax.ppermute(grad_send, "core", SWAP)

    left2 = lax.ppermute(after(left, grad_send), "core", SWAP)

    left_wide, left_tall = vmem_call(
        left_forms, (shaped(2 * rank, rows, dtype=BF16), shaped(rows, 2 * rank, dtype=BF16)), left, left2
    )
    inverse = vmem_call(inverse_factor, shaped(rank, rank), left, left2, flops=12 * rank * rank * rows)
    merged_t, right = vmem_call(
        merge,
        (shaped(own, rows), shaped(reps, rank, own)),
        grad_keep,
        grad_in,
        left_wide,
        flops=6 * rank * own * rows,
    )
    right = direct(right, "rep")
    merged = vmem_call(turn, shaped(rows, own), merged_t)
    approx, new_error, q_new = finished(right, inverse, left_tall, merged)
    return approx, new_error[None], q_new.T


def solution(mesh):
    return build(mesh, (8, 4, 8, 2))


def build(mesh, shape):
    names = ("rep", "x", "z", "core")
    grid = Mesh(mesh.devices.reshape(shape), names)
    sizes = dict(zip(names, shape))
    shard = ("x", "z", "core")
    placed = (
        P("rep", shard, None),
        P("rep", shard, None),
        P("rep", None, shard),
        P(shard, None),
    )
    return jax.shard_map(
        lambda *args: per_device(sizes, *args),
        mesh=grid,
        in_specs=placed,
        out_specs=(P(None, shard), P("rep", None, shard), P(shard, None)),
        check_vma=False,
    )
```

time: 176 us -> 184 us (1.045)
  starting transfers between devices: 39.9 us -> 54.8 us
  local copies, waits for them, and re-layouts: 15 us -> 8.65 us
  blocking collectives: 47.5 us -> 49.9 us
  Pallas kernels: 20.6 us -> 18.5 us
    all_to_all x4 -> x3, waiting for transfers between devices: 31 us -> 3.7 us  [direct(): return lax.all_to_all(blocks, axes, split_axis=0, concat_axis=0, tiled=True)]
    ppermute x1 -> x9, starting transfers between devices: 3 us -> 29.2 us  [the longest x6 19.8 us: shifted(): lax.ppermute(value, 'x', [(i, (i + shift) % across) for i in range(across)])]
    ppermute x1 -> x9, waiting for transfers between devices: 0.84 us -> 15 us  [the longest x6 12.9 us: shifted(): lax.ppermute(value, 'x', [(i, (i + shift) % across) for i in range(across)])]
    all_gather x1, waiting for transfers between devices: 4.49 us -> 17.8 us  [per_device(): gathered = lax.all_gather(tokens, ('x', 'z'), axis=0, tiled=True)]
    all_to_all x4 -> x3, starting transfers between devices: 33.8 us -> 23.1 us  [direct(): return lax.all_to_all(blocks, axes, split_axis=0, concat_axis=0, tiled=True)]
    pallas_call x2 -> x0, Pallas kernels: 6.15 us -> none  [turned_grad(): pl.pallas_call(columns_product, out_shape=shaped(own, rows), grid=(rows /...]
    unnamed x26 -> x18, local copies, waits for them, and re-layouts: 12 us -> 8.65 us
    pallas_call x7 -> x14, Pallas kernels: 11 us -> 13.7 us  [vmem_call(): pl.pallas_call(body, out_shape=out_shape, in_specs=[whole] * len(args), o...]
  transfers between devices with their start and end apart: 7 -> 14, of which waited for: 6 -> 7; matrix products, arithmetic and copies ran while one was open for 2% -> 0% of each run, Pallas kernels for 9% -> 6%
where the time goes in v2:
time: 184 us; the launch traced here: 183 us
  starting transfers between devices  54.8 us (30%)
  blocking collectives  49.9 us (27%)
  waiting for transfers between devices  37.2 us (20%)
  Pallas kernels  18.5 us (10%)
  between operations  14.3 us (8%)
  local copies, waits for them, and re-layouts  8.65 us (5%)
    all_to_all x3, blocking collectives, direct(): return lax.all_to_all(blocks, axes, split_axis=0, concat_axis=0, tiled=True)  49.9 us
    all_to_all x3, starting transfers between devices, direct(): return lax.all_to_all(blocks, axes, split_axis=0, concat_axis=0, tiled=True)  23.1 us
    ppermute x6, starting transfers between devices, shifted(): lax.ppermute(value, 'x', [(i, (i + shift) % across) for i in range(across)])  19.8 us
    all_gather x1, waiting for transfers between devices, per_device(): gathered = lax.all_gather(tokens, ('x', 'z'), axis=0, tiled=True)  17.8 us
    pallas_call x14, Pallas kernels, vmem_call(): pl.pallas_call(body, out_shape=out_shape, in_specs=[whole] * len(args), o...  13.7 us
    ppermute x6, waiting for transfers between devices, shifted(): lax.ppermute(value, 'x', [(i, (i + shift) % across) for i in range(across)])  12.9 us
    unnamed x18, local copies, waits for them, and re-layouts  8.65 us
    pallas_call x1, Pallas kernels, finished(): pl.pallas_call(finish, out_shape=outs, grid=(rows // step,), in_specs=[pl...  4.76 us
  transfers between devices with their start and end apart: 14, of which 7 were waited for; matrix products, arithmetic and copies ran while one was open for 0% of the time, Pallas kernels for 6%

profile of v2, /device:TPU:1, one launch (start us, length us, event | category | flops | bytes accessed | tf_op | source)
XLA Modules:
  0.0 183.4 jit_solution(16716492404399510500)
XLA Ops:
  9.8 10.9 %all-to-all-start = ((bf16[8,8,32,128]{3,2,1,0:T(8,128)(2,1)}), bf16[8,8,32,128]{3,2,1,0:T(8,128)(2,1)S(1)}, u32[]{:S(2)}, u32[]{:S(2)}) async-start(bf16[8,8,32,128]{3,2,1,0:T(8,128)(2,1)} %shard_map.67), calls=%async_computation | async-start | bytes 1048576 | tf_op jit(solution)/shard_map/all_to_all | solution.py:304
  20.7 2.9 %collective-permute-start = (f32[64,128]{1,0:T(8,128)S(1)}, f32[64,128]{1,0:T(8,128)S(1)}, u32[]{:S(2)}, u32[]{:S(2)}) collective-permute-start(f32[64,128]{1,0:T(8,128)S(1)} %bitcast.13), channel_id=1, source_target_pairs={{0,1},{1,0},{2,3},{3,2},{4,5},{5,4},{6,7},{7,6},{8,9},{9,8},{10,11... | collective-permute-start | bytes 98312 | tf_op jit(solution)/shard_map/ppermute | solution.py:328
  24.4 4.4 %collective-permute-start.3 = (f32[2,64,128]{2,1,0:T(8,128)S(1)}, f32[2,64,128]{2,1,0:T(8,128)S(1)}, u32[]{:S(2)}, u32[]{:S(2)}) collective-permute-start(f32[2,64,128]{2,1,0:T(8,128)S(1)} %pad_maximum_fusion.refs_0_), channel_id=1, source_target_pairs={{0,48},{16,0},{32,16},{48,32},{1,49},{17,1},{33,17},{49,33},{2,50}... | collective-permute-start | bytes 196616 | tf_op jit(solution)/shard_map/ppermute | solution.py:308
  28.8 2.4 %collective-permute-start.2 = (f32[2,64,128]{2,1,0:T(8,128)S(1)}, f32[2,64,128]{2,1,0:T(8,128)S(1)}, u32[]{:S(2)}, u32[]{:S(2)}) collective-permute-start(f32[2,64,128]{2,1,0:T(8,128)S(1)} %pad_maximum_fusion.refs_0_), channel_id=1, source_target_pairs={{0,32},{16,48},{32,0},{48,16},{1,33},{17,49},{33,1},{49,17},{2,34}... | collective-permute-start | bytes 196616 | tf_op jit(solution)/shard_map/ppermute | solution.py:308
  31.2 2.5 %collective-permute-start.1 = (f32[2,64,128]{2,1,0:T(8,128)S(1)}, f32[2,64,128]{2,1,0:T(8,128)S(1)}, u32[]{:S(2)}, u32[]{:S(2)}) collective-permute-start(f32[2,64,128]{2,1,0:T(8,128)S(1)} %pad_maximum_fusion.refs_0_), channel_id=1, source_target_pairs={{0,16},{16,32},{32,48},{48,0},{1,17},{17,33},{33,49},{49,1},{2,18}... | collective-permute-start | bytes 196616 | tf_op jit(solution)/shard_map/ppermute | solution.py:308
  36.0 2.8 %collective-permute-done.1.refs_1_ = f32[2,64,128]{2,1,0:T(8,128)S(1)} collective-permute-done((f32[2,64,128]{2,1,0:T(8,128)S(1)}, f32[2,64,128]{2,1,0:T(8,128)S(1)}, u32[]{:S(2)}, u32[]{:S(2)}) %collective-permute-start.1) | collective-permute-done | bytes 65568 | tf_op jit(solution)/shard_map/ppermute | solution.py:308
  39.2 2.8 %collective-permute-start.4 = (f32[96,3072]{1,0:T(8,128)S(1)}, f32[96,3072]{1,0:T(8,128)S(1)}, u32[]{:S(2)}, u32[]{:S(2)}) collective-permute-start(f32[96,3072]{1,0:T(8,128)S(1)} %get-tuple-element.28.add_ref), channel_id=1, source_target_pairs={{0,1},{1,0},{2,3},{3,2},{4,5},{5,4},{6,7},{7,6},{8,9},{9,8},{10,11... | collective-permute-start | bytes 3538952 | tf_op jit(solution)/shard_map/ppermute | solution.py:346
  42.0 16.1 %all_to_all.30.y_ref = f32[16,16,128]{2,1,0:T(8,128)S(1)} all-to-all(f32[16,16,128]{2,1,0:T(8,128)S(1)} %shard_map.69), channel_id=1, replica_groups=mesh['rep'=8,'x'=4,'z'=8,'core'=2] {'z','core'}, dimensions={0} | all-to-all | bytes 262144 | tf_op jit(solution)/shard_map/all_to_all | solution.py:304
  59.3 8.8 %all-to-all-start.2 = ((f32[32,8,384]{2,1,0:T(8,128)}), f32[32,8,384]{2,1,0:T(8,128)S(1)}, u32[]{:S(2)}, u32[]{:S(2)}) async-start(f32[32,8,384]{2,1,0:T(8,128)} %shard_map.71), calls=%async_computation.2 | async-start | bytes 786432 | tf_op jit(solution)/shard_map/all_to_all | solution.py:304
  68.2 3.1 %collective-permute-start.5 = (bf16[8,2,32,128]{3,2,1,0:T(8,128)(2,1)S(1)}, bf16[8,2,32,128]{3,2,1,0:T(8,128)(2,1)S(1)}, u32[]{:S(2)}, u32[]{:S(2)}) collective-permute-start(bf16[8,2,32,128]{3,2,1,0:T(8,128)(2,1)S(1)} %get-tuple-element.31), channel_id=1, source_target_pairs={{0,16},{16,32},{32,48},{48,0},{1,17},{17,33},{33,49},{49,1},{2,18}... | collective-permute-start | bytes 393224 | tf_op jit(solution)/shard_map/ppermute | solution.py:308
  71.3 4.3 %collective-permute-start.6 = (bf16[8,2,32,128]{3,2,1,0:T(8,128)(2,1)S(1)}, bf16[8,2,32,128]{3,2,1,0:T(8,128)(2,1)S(1)}, u32[]{:S(2)}, u32[]{:S(2)}) collective-permute-start(bf16[8,2,32,128]{3,2,1,0:T(8,128)(2,1)S(1)} %get-tuple-element.32), channel_id=1, source_target_pairs={{0,32},{16,48},{32,0},{48,16},{1,33},{17,49},{33,1},{49,17},{2,34}... | collective-permute-start | bytes 393224 | tf_op jit(solution)/shard_map/ppermute | solution.py:308
  75.7 3.1 %collective-permute-start.7 = (bf16[8,2,32,128]{3,2,1,0:T(8,128)(2,1)S(1)}, bf16[8,2,32,128]{3,2,1,0:T(8,128)(2,1)S(1)}, u32[]{:S(2)}, u32[]{:S(2)}) collective-permute-start(bf16[8,2,32,128]{3,2,1,0:T(8,128)(2,1)S(1)} %get-tuple-element.33), channel_id=1, source_target_pairs={{0,48},{16,0},{32,16},{48,32},{1,49},{17,1},{33,17},{49,33},{2,50}... | collective-permute-start | bytes 393224 | tf_op jit(solution)/shard_map/ppermute | solution.py:308
  78.8 7.4 %collective-permute-done.6.refs_2_ = bf16[8,2,32,128]{3,2,1,0:T(8,128)(2,1)S(1)} collective-permute-done((bf16[8,2,32,128]{3,2,1,0:T(8,128)(2,1)S(1)}, bf16[8,2,32,128]{3,2,1,0:T(8,128)(2,1)S(1)}, u32[]{:S(2)}, u32[]{:S(2)}) %collective-permute-start.6) | collective-permute-done | bytes 131104 | tf_op jit(solution)/shard_map/ppermute | solution.py:308
  86.2 2.6 %collective-permute-done.7.refs_3_ = bf16[8,2,32,128]{3,2,1,0:T(8,128)(2,1)S(1)} collective-permute-done((bf16[8,2,32,128]{3,2,1,0:T(8,128)(2,1)S(1)}, bf16[8,2,32,128]{3,2,1,0:T(8,128)(2,1)S(1)}, u32[]{:S(2)}, u32[]{:S(2)}) %collective-permute-start.7) | collective-permute-done | bytes 131104 | tf_op jit(solution)/shard_map/ppermute | solution.py:308
  89.0 11.1 %all_to_all.31.in_ref = f32[8,8,384]{2,1,0:T(8,128)S(1)} all-to-all(f32[8,8,384]{2,1,0:T(8,128)S(1)} %shard_map.74), channel_id=1, replica_groups=mesh['rep'=8,'x'=4,'z'=8,'core'=2] {'z'}, dimensions={0} | all-to-all | bytes 196608 | tf_op jit(solution)/shard_map/all_to_all | solution.py:304
  100.2 17.8 %all-gather.3.cloned.1.call-done = bf16[1,1024,3072]{2,1,0:T(8,128)(2,1)} async-done(((bf16[1,32,3072]{2,1,0:T(8,128)(2,1)}), bf16[1,1024,3072]{2,1,0:T(8,128)(2,1)}) %all-gather.3.cloned.1.call-update) | async-done | bytes 6291472 | tf_op jit(solution)/shard_map/all_gather | solution.py:323
  118.0 2.8 %copy-done = bf16[1,1024,3072]{2,1,0:T(8,128)(2,1)S(1)} copy-done((bf16[1,1024,3072]{2,1,0:T(8,128)(2,1)S(1)}, bf16[1,1024,3072]{2,1,0:T(8,128)(2,1)}, u32[]{:S(2)}) %copy-start) | copy-done | bytes 6291480
  122.6 2.5 %collective-permute-start.8 = (f32[128,3072]{1,0:T(8,128)S(1)}, f32[128,3072]{1,0:T(8,128)S(1)}, u32[]{:S(2)}, u32[]{:S(2)}) collective-permute-start(f32[128,3072]{1,0:T(8,128)S(1)} %get-tuple-element.38), channel_id=1, source_target_pairs={{0,1},{1,0},{2,3},{3,2},{4,5},{5,4},{6,7},{7,6},{8,9},{9,8},{10,11... | collective-permute-start | bytes 4718600 | tf_op jit(solution)/shard_map/ppermute | solution.py:379
  125.0 22.7 %all_to_all.32.mine_ref = f32[32,8,384]{2,1,0:T(8,128)S(1)} all-to-all(f32[32,8,384]{2,1,0:T(8,128)S(1)} %shard_map.75), channel_id=1, replica_groups=mesh['rep'=8,'x'=4,'z'=8,'core'=2] {'rep','x'}, dimensions={0} | all-to-all | bytes 786432 | tf_op jit(solution)/shard_map/all_to_all | solution.py:304
  147.7 3.7 %collective-permute-start.9 = (f32[32,8,384]{2,1,0:T(8,128)S(1)}, f32[32,8,384]{2,1,0:T(8,128)S(1)}, u32[]{:S(2)}, u32[]{:S(2)}) collective-permute-start(f32[32,8,384]{2,1,0:T(8,128)S(1)} %all_to_all.32.mine_ref), channel_id=1, source_target_pairs={{0,1},{1,0},{2,3},{3,2},{4,5},{5,4},{6,7},{7,6},{8,9},{9,8},{10,11... | collective-permute-start | bytes 1179656 | tf_op jit(solution)/shard_map/ppermute | solution.py:381
  155.4 3.4 %all-to-all-start.5 = ((f32[8,64,128]{2,1,0:T(8,128)}), f32[8,64,128]{2,1,0:T(8,128)S(1)}, u32[]{:S(2)}, u32[]{:S(2)}) async-start(f32[8,64,128]{2,1,0:T(8,128)} %get-tuple-element.41), calls=%async_computation.5 | async-start | bytes 524288 | tf_op jit(solution)/shard_map/all_to_all | solution.py:304
  158.8 6.3 %shard_map.79.inverse_ref = f32[64,64]{1,0:T(8,128)S(1)} custom-call(f32[32,8,384]{2,1,0:T(8,128)S(1)} %all_to_all.32.mine_ref, f32[32,8,384]{2,1,0:T(8,128)S(1)} %collective-permute-done.9.other_ref), custom_call_target="tpu_custom_call" | custom-call | flops 150994944 | bytes 802816 | tf_op jit(solution)/shard_map/pallas_call | solution.py:53
  167.3 3.7 %all-to-all-done.5.right_ref = f32[8,64,128]{2,1,0:T(8,128)S(1)} async-done(((f32[8,64,128]{2,1,0:T(8,128)}), f32[8,64,128]{2,1,0:T(8,128)S(1)}, u32[]{:S(2)}, u32[]{:S(2)}) %all-to-all-start.5) | async-done | bytes 262176 | tf_op jit(solution)/shard_map/all_to_all | solution.py:304
  171.8 4.8 %shard_map.81 = (bf16[3072,128]{1,0:T(8,128)(2,1)}, f32[3072,128]{1,0:T(8,128)}, f32[64,128]{1,0:T(8,128)}) custom-call(f32[8,64,128]{2,1,0:T(8,128)} %copy-done.8, f32[64,64]{1,0:T(8,128)} %copy-done.7, bf16[3072,128]{1,0:T(8,128)(2,1)} %copy-done.4, f32[3072,128]{1,0:T(8,128)} %copy-done.1), custom_call_target="tpu_custom_call" | custom-call | flops 150994944 | bytes 5013504 | tf_op jit(solution)/shard_map/pallas_call | solution.py:282
  (42 shorter events, 16.2 us)
Async XLA Ops:
  7.2 26.6 %copy-start.3 = (bf16[1,32,3072]{2,1,0:T(8,128)(2,1)S(1)}, bf16[1,32,3072]{2,1,0:T(8,128)(2,1)}, u32[]{:S(2)}) copy-start(bf16[1,32,3072]{2,1,0:T(8,128)(2,1)} %param.4) | copy-start | bytes 589828
  7.2 110.8 %all-gather.3.cloned.1.call-start = ((), (), s32[]{:S(2)}) async-start(), calls=%async_computation.6 | async-start | bytes 6488064 | tf_op jit(solution)/shard_map/all_gather | solution.py:323
  7.9 1.0 copy-start.5
  9.0 11.8 %copy-start.6 = (f32[128,64]{0,1:T(8,128)S(1)}, f32[128,64]{0,1:T(8,128)}, u32[]{:S(2)}) copy-start(f32[128,64]{0,1:T(8,128)} %param.7) | copy-start | bytes 98308
  9.8 29.0 %all-to-all-start = ((bf16[8,8,32,128]{3,2,1,0:T(8,128)(2,1)}), bf16[8,8,32,128]{3,2,1,0:T(8,128)(2,1)S(1)}, u32[]{:S(2)}, u32[]{:S(2)}) async-start(bf16[8,8,32,128]{3,2,1,0:T(8,128)(2,1)} %shard_map.67), calls=%async_computation | async-start | bytes 1048576 | tf_op jit(solution)/shard_map/all_to_all | solution.py:304
  20.7 3.7 %collective-permute-start = (f32[64,128]{1,0:T(8,128)S(1)}, f32[64,128]{1,0:T(8,128)S(1)}, u32[]{:S(2)}, u32[]{:S(2)}) collective-permute-start(f32[64,128]{1,0:T(8,128)S(1)} %bitcast.13), channel_id=1, source_target_pairs={{0,1},{1,0},{2,3},{3,2},{4,5},{5,4},{6,7},{7,6},{8,9},{9,8},{10,11... | collective-permute-start | bytes 98312 | tf_op jit(solution)/shard_map/ppermute | solution.py:328
  24.4 11.5 %collective-permute-start.3 = (f32[2,64,128]{2,1,0:T(8,128)S(1)}, f32[2,64,128]{2,1,0:T(8,128)S(1)}, u32[]{:S(2)}, u32[]{:S(2)}) collective-permute-start(f32[2,64,128]{2,1,0:T(8,128)S(1)} %pad_maximum_fusion.refs_0_), channel_id=1, source_target_pairs={{0,48},{16,0},{32,16},{48,32},{1,49},{17,1},{33,17},{49,33},{2,50}... | collective-permute-start | bytes 196616 | tf_op jit(solution)/shard_map/ppermute | solution.py:308
  28.8 7.1 %collective-permute-start.2 = (f32[2,64,128]{2,1,0:T(8,128)S(1)}, f32[2,64,128]{2,1,0:T(8,128)S(1)}, u32[]{:S(2)}, u32[]{:S(2)}) collective-permute-start(f32[2,64,128]{2,1,0:T(8,128)S(1)} %pad_maximum_fusion.refs_0_), channel_id=1, source_target_pairs={{0,32},{16,48},{32,0},{48,16},{1,33},{17,49},{33,1},{49,17},{2,34}... | collective-permute-start | bytes 196616 | tf_op jit(solution)/shard_map/ppermute | solution.py:308
  31.2 7.6 %collective-permute-start.1 = (f32[2,64,128]{2,1,0:T(8,128)S(1)}, f32[2,64,128]{2,1,0:T(8,128)S(1)}, u32[]{:S(2)}, u32[]{:S(2)}) collective-permute-start(f32[2,64,128]{2,1,0:T(8,128)S(1)} %pad_maximum_fusion.refs_0_), channel_id=1, source_target_pairs={{0,16},{16,32},{32,48},{48,0},{1,17},{17,33},{33,49},{49,1},{2,18}... | collective-permute-start | bytes 196616 | tf_op jit(solution)/shard_map/ppermute | solution.py:308
  33.8 1.4 copy-start.2
  39.2 18.9 %collective-permute-start.4 = (f32[96,3072]{1,0:T(8,128)S(1)}, f32[96,3072]{1,0:T(8,128)S(1)}, u32[]{:S(2)}, u32[]{:S(2)}) collective-permute-start(f32[96,3072]{1,0:T(8,128)S(1)} %get-tuple-element.28.add_ref), channel_id=1, source_target_pairs={{0,1},{1,0},{2,3},{3,2},{4,5},{5,4},{6,7},{7,6},{8,9},{9,8},{10,11... | collective-permute-start | bytes 3538952 | tf_op jit(solution)/shard_map/ppermute | solution.py:346
  59.3 29.7 %all-to-all-start.2 = ((f32[32,8,384]{2,1,0:T(8,128)}), f32[32,8,384]{2,1,0:T(8,128)S(1)}, u32[]{:S(2)}, u32[]{:S(2)}) async-start(f32[32,8,384]{2,1,0:T(8,128)} %shard_map.71), calls=%async_computation.2 | async-start | bytes 786432 | tf_op jit(solution)/shard_map/all_to_all | solution.py:304
  68.2 10.6 %collective-permute-start.5 = (bf16[8,2,32,128]{3,2,1,0:T(8,128)(2,1)S(1)}, bf16[8,2,32,128]{3,2,1,0:T(8,128)(2,1)S(1)}, u32[]{:S(2)}, u32[]{:S(2)}) collective-permute-start(bf16[8,2,32,128]{3,2,1,0:T(8,128)(2,1)S(1)} %get-tuple-element.31), channel_id=1, source_target_pairs={{0,16},{16,32},{32,48},{48,0},{1,17},{17,33},{33,49},{49,1},{2,18}... | collective-permute-start | bytes 393224 | tf_op jit(solution)/shard_map/ppermute | solution.py:308
  71.3 14.8 %collective-permute-start.6 = (bf16[8,2,32,128]{3,2,1,0:T(8,128)(2,1)S(1)}, bf16[8,2,32,128]{3,2,1,0:T(8,128)(2,1)S(1)}, u32[]{:S(2)}, u32[]{:S(2)}) collective-permute-start(bf16[8,2,32,128]{3,2,1,0:T(8,128)(2,1)S(1)} %get-tuple-element.32), channel_id=1, source_target_pairs={{0,32},{16,48},{32,0},{48,16},{1,33},{17,49},{33,1},{49,17},{2,34}... | collective-permute-start | bytes 393224 | tf_op jit(solution)/shard_map/ppermute | solution.py:308
  75.7 13.1 %collective-permute-start.7 = (bf16[8,2,32,128]{3,2,1,0:T(8,128)(2,1)S(1)}, bf16[8,2,32,128]{3,2,1,0:T(8,128)(2,1)S(1)}, u32[]{:S(2)}, u32[]{:S(2)}) collective-permute-start(bf16[8,2,32,128]{3,2,1,0:T(8,128)(2,1)S(1)} %get-tuple-element.33), channel_id=1, source_target_pairs={{0,48},{16,0},{32,16},{48,32},{1,49},{17,1},{33,17},{49,33},{2,50}... | collective-permute-start | bytes 393224 | tf_op jit(solution)/shard_map/ppermute | solution.py:308
  118.0 2.8 %copy-start = (bf16[1,1024,3072]{2,1,0:T(8,128)(2,1)S(1)}, bf16[1,1024,3072]{2,1,0:T(8,128)(2,1)}, u32[]{:S(2)}) copy-start(bf16[1,1024,3072]{2,1,0:T(8,128)(2,1)} %all-gather.3.cloned.1.call-done) | copy-start | bytes 18874372
  122.6 31.4 %collective-permute-start.8 = (f32[128,3072]{1,0:T(8,128)S(1)}, f32[128,3072]{1,0:T(8,128)S(1)}, u32[]{:S(2)}, u32[]{:S(2)}) collective-permute-start(f32[128,3072]{1,0:T(8,128)S(1)} %get-tuple-element.38), channel_id=1, source_target_pairs={{0,1},{1,0},{2,3},{3,2},{4,5},{5,4},{6,7},{7,6},{8,9},{9,8},{10,11... | collective-permute-start | bytes 4718600 | tf_op jit(solution)/shard_map/ppermute | solution.py:379
  147.7 5.0 %collective-permute-start.9 = (f32[32,8,384]{2,1,0:T(8,128)S(1)}, f32[32,8,384]{2,1,0:T(8,128)S(1)}, u32[]{:S(2)}, u32[]{:S(2)}) collective-permute-start(f32[32,8,384]{2,1,0:T(8,128)S(1)} %all_to_all.32.mine_ref), channel_id=1, source_target_pairs={{0,1},{1,0},{2,3},{3,2},{4,5},{5,4},{6,7},{7,6},{8,9},{9,8},{10,11... | collective-permute-start | bytes 1179656 | tf_op jit(solution)/shard_map/ppermute | solution.py:381
  153.1 0.9 copy-start.4
  155.4 15.7 %all-to-all-start.5 = ((f32[8,64,128]{2,1,0:T(8,128)}), f32[8,64,128]{2,1,0:T(8,128)S(1)}, u32[]{:S(2)}, u32[]{:S(2)}) async-start(f32[8,64,128]{2,1,0:T(8,128)} %get-tuple-element.41), calls=%async_computation.5 | async-start | bytes 524288 | tf_op jit(solution)/shard_map/all_to_all | solution.py:304
  165.1 0.6 copy-start.7
  166.2 1.2 copy-start.1
  171.0 0.7 copy-start.8
Sparse Core Ops, SparseCore 0:
  11.2 106.7 all-gather.2

commit v3 on v2

--- a/solution.py
+++ b/solution.py
@@ -296,7 +296,7 @@
         ),
         scratch_shapes=[pltpu.VMEM((2 * rank, 2 * own), BF16)],
         cost_estimate=cost(6 * rows * rank * own, [right, left, merged] + list(outs)),
-        compiler_params=pltpu.CompilerParams(vmem_limit_bytes=60 << 20),
+        compiler_params=pltpu.CompilerParams(vmem_limit_bytes=16 << 20),
     )(right, inverse, left, merged)
 
 
@@ -367,7 +367,7 @@
     left = direct(left, "z")
     summed = vmem_call(add_spread, shaped(peers, 8, width), left)
     left = direct(summed, PEERS)
-    gathered = after(gathered, summed)
+    gathered = after(gathered, left)
     grad_keep, grad_send = vmem_call(
         turned_grad,
         (shaped(own, rows), shaped(own, rows)),
@@ -378,7 +378,7 @@
     )
     grad_in = lax.ppermute(grad_send, "core", SWAP)
 
-    left2 = lax.ppermute(after(left, grad_send), "core", SWAP)
+    left2 = lax.ppermute(left, "core", SWAP)
 
     left_wide, left_tall = vmem_call(
         left_forms, (shaped(2 * rank, rows, dtype=BF16), shaped(rows, 2 * rank, dtype=BF16)), left, left2

time: 184 us -> 167 us (0.908)
  waiting for transfers between devices: 37.2 us -> 21 us
  starting transfers between devices: 54.8 us -> 58.2 us
  blocking collectives: 49.9 us -> 47.2 us
    all_gather x1, waiting for transfers between devices: 17.8 us -> 0.01 us  [per_device(): gathered = lax.all_gather(tokens, ('x', 'z'), axis=0, tiled=True)]
    ppermute x1, starting transfers between devices: 2.46 us -> 7.14 us  [per_device(): grad_in = lax.ppermute(grad_send, 'core', SWAP)]
    all_to_all x3, blocking collectives: 49.9 us -> 47.2 us  [direct(): return lax.all_to_all(blocks, axes, split_axis=0, concat_axis=0, tiled=True)]
  transfers between devices with their start and end apart: 14 -> 14, of which waited for: 7 -> 6; matrix products, arithmetic and copies ran while one was open for 0% -> 0% of each run, Pallas kernels for 6% -> 6%
where the time goes in v3:
time: 167 us; the launch traced here: 166 us
  starting transfers between devices  58.2 us (35%)
  blocking collectives  47.2 us (28%)
  waiting for transfers between devices  21 us (13%)
  Pallas kernels  17.4 us (10%)
  between operations  14.3 us (9%)
  local copies, waits for them, and re-layouts  7.86 us (5%)
    all_to_all x3, blocking collectives, direct(): return lax.all_to_all(blocks, axes, split_axis=0, concat_axis=0, tiled=True)  47.2 us
    all_to_all x3, starting transfers between devices, direct(): return lax.all_to_all(blocks, axes, split_axis=0, concat_axis=0, tiled=True)  23.6 us
    ppermute x6, starting transfers between devices, shifted(): lax.ppermute(value, 'x', [(i, (i + shift) % across) for i in range(across)])  19.8 us
    pallas_call x14, Pallas kernels, vmem_call(): pl.pallas_call(body, out_shape=out_shape, in_specs=[whole] * len(args), o...  13.7 us
    ppermute x6, waiting for transfers between devices, shifted(): lax.ppermute(value, 'x', [(i, (i + shift) % across) for i in range(across)])  12.8 us
    unnamed x18, local copies, waits for them, and re-layouts  7.86 us
    ppermute x1, starting transfers between devices, per_device(): grad_in = lax.ppermute(grad_send, 'core', SWAP)  7.14 us
    all_to_all x3, waiting for transfers between devices, direct(): return lax.all_to_all(blocks, axes, split_axis=0, concat_axis=0, tiled=True)  4.96 us
  transfers between devices with their start and end apart: 14, of which 6 were waited for; matrix products, arithmetic and copies ran while one was open for 0% of the time, Pallas kernels for 6%

profile of v3, /device:TPU:1, one launch (start us, length us, event | category | flops | bytes accessed | tf_op | source)
XLA Modules:
  0.0 166.0 jit_solution(7051217712217107912)
XLA Ops:
  9.8 10.9 %all-to-all-start = ((bf16[8,8,32,128]{3,2,1,0:T(8,128)(2,1)}), bf16[8,8,32,128]{3,2,1,0:T(8,128)(2,1)S(1)}, u32[]{:S(2)}, u32[]{:S(2)}) async-start(bf16[8,8,32,128]{3,2,1,0:T(8,128)(2,1)} %shard_map.67), calls=%async_computation | async-start | bytes 1048576 | tf_op jit(solution)/shard_map/all_to_all | solution.py:304
  20.7 2.9 %collective-permute-start = (f32[64,128]{1,0:T(8,128)S(1)}, f32[64,128]{1,0:T(8,128)S(1)}, u32[]{:S(2)}, u32[]{:S(2)}) collective-permute-start(f32[64,128]{1,0:T(8,128)S(1)} %bitcast.13), channel_id=1, source_target_pairs={{0,1},{1,0},{2,3},{3,2},{4,5},{5,4},{6,7},{7,6},{8,9},{9,8},{10,11... | collective-permute-start | bytes 98312 | tf_op jit(solution)/shard_map/ppermute | solution.py:328
  24.4 4.4 %collective-permute-start.3 = (f32[2,64,128]{2,1,0:T(8,128)S(1)}, f32[2,64,128]{2,1,0:T(8,128)S(1)}, u32[]{:S(2)}, u32[]{:S(2)}) collective-permute-start(f32[2,64,128]{2,1,0:T(8,128)S(1)} %pad_maximum_fusion.refs_0_), channel_id=1, source_target_pairs={{0,48},{16,0},{32,16},{48,32},{1,49},{17,1},{33,17},{49,33},{2,50}... | collective-permute-start | bytes 196616 | tf_op jit(solution)/shard_map/ppermute | solution.py:308
  28.8 2.4 %collective-permute-start.2 = (f32[2,64,128]{2,1,0:T(8,128)S(1)}, f32[2,64,128]{2,1,0:T(8,128)S(1)}, u32[]{:S(2)}, u32[]{:S(2)}) collective-permute-start(f32[2,64,128]{2,1,0:T(8,128)S(1)} %pad_maximum_fusion.refs_0_), channel_id=1, source_target_pairs={{0,32},{16,48},{32,0},{48,16},{1,33},{17,49},{33,1},{49,17},{2,34}... | collective-permute-start | bytes 196616 | tf_op jit(solution)/shard_map/ppermute | solution.py:308
  31.2 2.5 %collective-permute-start.1 = (f32[2,64,128]{2,1,0:T(8,128)S(1)}, f32[2,64,128]{2,1,0:T(8,128)S(1)}, u32[]{:S(2)}, u32[]{:S(2)}) collective-permute-start(f32[2,64,128]{2,1,0:T(8,128)S(1)} %pad_maximum_fusion.refs_0_), channel_id=1, source_target_pairs={{0,16},{16,32},{32,48},{48,0},{1,17},{17,33},{33,49},{49,1},{2,18}... | collective-permute-start | bytes 196616 | tf_op jit(solution)/shard_map/ppermute | solution.py:308
  36.0 2.8 %collective-permute-done.1.refs_1_ = f32[2,64,128]{2,1,0:T(8,128)S(1)} collective-permute-done((f32[2,64,128]{2,1,0:T(8,128)S(1)}, f32[2,64,128]{2,1,0:T(8,128)S(1)}, u32[]{:S(2)}, u32[]{:S(2)}) %collective-permute-start.1) | collective-permute-done | bytes 65568 | tf_op jit(solution)/shard_map/ppermute | solution.py:308
  39.2 2.8 %collective-permute-start.4 = (f32[96,3072]{1,0:T(8,128)S(1)}, f32[96,3072]{1,0:T(8,128)S(1)}, u32[]{:S(2)}, u32[]{:S(2)}) collective-permute-start(f32[96,3072]{1,0:T(8,128)S(1)} %get-tuple-element.27.add_ref), channel_id=1, source_target_pairs={{0,1},{1,0},{2,3},{3,2},{4,5},{5,4},{6,7},{7,6},{8,9},{9,8},{10,11... | collective-permute-start | bytes 3538952 | tf_op jit(solution)/shard_map/ppermute | solution.py:346
  42.0 16.1 %all_to_all.30.y_ref = f32[16,16,128]{2,1,0:T(8,128)S(1)} all-to-all(f32[16,16,128]{2,1,0:T(8,128)S(1)} %shard_map.69), channel_id=1, replica_groups=mesh['rep'=8,'x'=4,'z'=8,'core'=2] {'z','core'}, dimensions={0} | all-to-all | bytes 262144 | tf_op jit(solution)/shard_map/all_to_all | solution.py:304
  59.3 8.7 %all-to-all-start.2 = ((f32[32,8,384]{2,1,0:T(8,128)}), f32[32,8,384]{2,1,0:T(8,128)S(1)}, u32[]{:S(2)}, u32[]{:S(2)}) async-start(f32[32,8,384]{2,1,0:T(8,128)} %shard_map.71), calls=%async_computation.2 | async-start | bytes 786432 | tf_op jit(solution)/shard_map/all_to_all | solution.py:304
  68.1 3.1 %collective-permute-start.5 = (bf16[8,2,32,128]{3,2,1,0:T(8,128)(2,1)S(1)}, bf16[8,2,32,128]{3,2,1,0:T(8,128)(2,1)S(1)}, u32[]{:S(2)}, u32[]{:S(2)}) collective-permute-start(bf16[8,2,32,128]{3,2,1,0:T(8,128)(2,1)S(1)} %get-tuple-element.30), channel_id=1, source_target_pairs={{0,16},{16,32},{32,48},{48,0},{1,17},{17,33},{33,49},{49,1},{2,18}... | collective-permute-start | bytes 393224 | tf_op jit(solution)/shard_map/ppermute | solution.py:308
  71.2 4.3 %collective-permute-start.6 = (bf16[8,2,32,128]{3,2,1,0:T(8,128)(2,1)S(1)}, bf16[8,2,32,128]{3,2,1,0:T(8,128)(2,1)S(1)}, u32[]{:S(2)}, u32[]{:S(2)}) collective-permute-start(bf16[8,2,32,128]{3,2,1,0:T(8,128)(2,1)S(1)} %get-tuple-element.31), channel_id=1, source_target_pairs={{0,32},{16,48},{32,0},{48,16},{1,33},{17,49},{33,1},{49,17},{2,34}... | collective-permute-start | bytes 393224 | tf_op jit(solution)/shard_map/ppermute | solution.py:308
  75.6 3.1 %collective-permute-start.7 = (bf16[8,2,32,128]{3,2,1,0:T(8,128)(2,1)S(1)}, bf16[8,2,32,128]{3,2,1,0:T(8,128)(2,1)S(1)}, u32[]{:S(2)}, u32[]{:S(2)}) collective-permute-start(bf16[8,2,32,128]{3,2,1,0:T(8,128)(2,1)S(1)} %get-tuple-element.32), channel_id=1, source_target_pairs={{0,48},{16,0},{32,16},{48,32},{1,49},{17,1},{33,17},{49,33},{2,50}... | collective-permute-start | bytes 393224 | tf_op jit(solution)/shard_map/ppermute | solution.py:308
  78.7 7.4 %collective-permute-done.6.refs_2_ = bf16[8,2,32,128]{3,2,1,0:T(8,128)(2,1)S(1)} collective-permute-done((bf16[8,2,32,128]{3,2,1,0:T(8,128)(2,1)S(1)}, bf16[8,2,32,128]{3,2,1,0:T(8,128)(2,1)S(1)}, u32[]{:S(2)}, u32[]{:S(2)}) %collective-permute-start.6) | collective-permute-done | bytes 131104 | tf_op jit(solution)/shard_map/ppermute | solution.py:308
  86.1 2.5 %collective-permute-done.7.refs_3_ = bf16[8,2,32,128]{3,2,1,0:T(8,128)(2,1)S(1)} collective-permute-done((bf16[8,2,32,128]{3,2,1,0:T(8,128)(2,1)S(1)}, bf16[8,2,32,128]{3,2,1,0:T(8,128)(2,1)S(1)}, u32[]{:S(2)}, u32[]{:S(2)}) %collective-permute-start.7) | collective-permute-done | bytes 131104 | tf_op jit(solution)/shard_map/ppermute | solution.py:308
  88.9 11.1 %all_to_all.31.in_ref = f32[8,8,384]{2,1,0:T(8,128)S(1)} all-to-all(f32[8,8,384]{2,1,0:T(8,128)S(1)} %shard_map.74), channel_id=1, replica_groups=mesh['rep'=8,'x'=4,'z'=8,'core'=2] {'z'}, dimensions={0} | all-to-all | bytes 196608 | tf_op jit(solution)/shard_map/all_to_all | solution.py:304
  100.0 20.0 %all_to_all.32.mine_ref = f32[32,8,384]{2,1,0:T(8,128)S(1)} all-to-all(f32[32,8,384]{2,1,0:T(8,128)S(1)} %shard_map.75), channel_id=1, replica_groups=mesh['rep'=8,'x'=4,'z'=8,'core'=2] {'rep','x'}, dimensions={0} | all-to-all | bytes 786432 | tf_op jit(solution)/shard_map/all_to_all | solution.py:304
  120.0 2.8 %copy-done = bf16[1,1024,3072]{2,1,0:T(8,128)(2,1)S(1)} copy-done((bf16[1,1024,3072]{2,1,0:T(8,128)(2,1)S(1)}, bf16[1,1024,3072]{2,1,0:T(8,128)(2,1)}, u32[]{:S(2)}) %copy-start) | copy-done | bytes 6291480
  122.8 1.8 %shard_map.76 = (f32[128,3072]{1,0:T(8,128)S(1)}, f32[128,3072]{1,0:T(8,128)S(1)}) custom-call(bf16[256,1024]{1,0:T(8,128)(2,1)S(1)} %shard_map.73.cols_ref, f32[128,3072]{1,0:T(8,128)S(1)} %get-tuple-element.33.e_ref, bf16[1024,3072]{1,0:T(8,128)(2,1)S(1)} %bitcast.9), custom_call_target="tpu_custom_call" | custom-call | flops 1610612736 | bytes 11534336 | tf_op jit(solution)/shard_map/pallas_call | solution.py:53
  124.5 7.1 %collective-permute-start.8 = (f32[128,3072]{1,0:T(8,128)S(1)}, f32[128,3072]{1,0:T(8,128)S(1)}, u32[]{:S(2)}, u32[]{:S(2)}) collective-permute-start(f32[128,3072]{1,0:T(8,128)S(1)} %get-tuple-element.37), channel_id=1, source_target_pairs={{0,1},{1,0},{2,3},{3,2},{4,5},{5,4},{6,7},{7,6},{8,9},{9,8},{10,11... | collective-permute-start | bytes 4718600 | tf_op jit(solution)/shard_map/ppermute | solution.py:379
  131.7 1.9 %collective-permute-start.9 = (f32[32,8,384]{2,1,0:T(8,128)S(1)}, f32[32,8,384]{2,1,0:T(8,128)S(1)}, u32[]{:S(2)}, u32[]{:S(2)}) collective-permute-start(f32[32,8,384]{2,1,0:T(8,128)S(1)} %all_to_all.32.mine_ref), channel_id=1, source_target_pairs={{0,1},{1,0},{2,3},{3,2},{4,5},{5,4},{6,7},{7,6},{8,9},{9,8},{10,11... | collective-permute-start | bytes 1179656 | tf_op jit(solution)/shard_map/ppermute | solution.py:381
  137.9 4.0 %all-to-all-start.5 = ((f32[8,64,128]{2,1,0:T(8,128)}), f32[8,64,128]{2,1,0:T(8,128)}, u32[]{:S(2)}, u32[]{:S(2)}) async-start(f32[8,64,128]{2,1,0:T(8,128)} %get-tuple-element.39), calls=%async_computation.5 | async-start | bytes 524288 | tf_op jit(solution)/shard_map/all_to_all | solution.py:304
  141.9 6.3 %shard_map.79.inverse_ref = f32[64,64]{1,0:T(8,128)S(1)} custom-call(f32[32,8,384]{2,1,0:T(8,128)S(1)} %all_to_all.32.mine_ref, f32[32,8,384]{2,1,0:T(8,128)S(1)} %collective-permute-done.9.other_ref), custom_call_target="tpu_custom_call" | custom-call | flops 150994944 | bytes 802816 | tf_op jit(solution)/shard_map/pallas_call | solution.py:53
  149.3 5.0 %all-to-all-done.5.right_ref = f32[8,64,128]{2,1,0:T(8,128)} async-done(((f32[8,64,128]{2,1,0:T(8,128)}), f32[8,64,128]{2,1,0:T(8,128)}, u32[]{:S(2)}, u32[]{:S(2)}) %all-to-all-start.5) | async-done | bytes 262176 | tf_op jit(solution)/shard_map/all_to_all | solution.py:304
  155.4 3.7 %shard_map.81 = (bf16[3072,128]{1,0:T(8,128)(2,1)}, f32[3072,128]{1,0:T(8,128)}, f32[64,128]{1,0:T(8,128)}) custom-call(f32[8,64,128]{2,1,0:T(8,128)} %all-to-all-done.5.right_ref, f32[64,64]{1,0:T(8,128)S(1)} %copy-done.8, bf16[3072,128]{1,0:T(8,128)(2,1)S(1)} %copy-done.4, f32[3072,128]{1,0:T(8,128)S(1)} %shard_map.80.merged_ref), custom_call_target="tpu_custom_call" | custom-call | flops 150994944 | bytes 5013504 | tf_op jit(solution)/shard_map/pallas_call | solution.py:282
  (42 shorter events, 14.0 us)
Async XLA Ops:
  7.2 26.6 %copy-start.2 = (bf16[1,32,3072]{2,1,0:T(8,128)(2,1)S(1)}, bf16[1,32,3072]{2,1,0:T(8,128)(2,1)}, u32[]{:S(2)}) copy-start(bf16[1,32,3072]{2,1,0:T(8,128)(2,1)} %param.4) | copy-start | bytes 589828
  7.2 112.8 %all-gather.3.cloned.1.call-start = ((), (), s32[]{:S(2)}) async-start(), calls=%async_computation.6 | async-start | bytes 6488064 | tf_op jit(solution)/shard_map/all_gather | solution.py:323
  7.9 1.0 copy-start.5
  9.0 11.8 %copy-start.6 = (f32[128,64]{0,1:T(8,128)S(1)}, f32[128,64]{0,1:T(8,128)}, u32[]{:S(2)}) copy-start(f32[128,64]{0,1:T(8,128)} %param.7) | copy-start | bytes 98308
  9.8 29.0 %all-to-all-start = ((bf16[8,8,32,128]{3,2,1,0:T(8,128)(2,1)}), bf16[8,8,32,128]{3,2,1,0:T(8,128)(2,1)S(1)}, u32[]{:S(2)}, u32[]{:S(2)}) async-start(bf16[8,8,32,128]{3,2,1,0:T(8,128)(2,1)} %shard_map.67), calls=%async_computation | async-start | bytes 1048576 | tf_op jit(solution)/shard_map/all_to_all | solution.py:304
  20.7 3.7 %collective-permute-start = (f32[64,128]{1,0:T(8,128)S(1)}, f32[64,128]{1,0:T(8,128)S(1)}, u32[]{:S(2)}, u32[]{:S(2)}) collective-permute-start(f32[64,128]{1,0:T(8,128)S(1)} %bitcast.13), channel_id=1, source_target_pairs={{0,1},{1,0},{2,3},{3,2},{4,5},{5,4},{6,7},{7,6},{8,9},{9,8},{10,11... | collective-permute-start | bytes 98312 | tf_op jit(solution)/shard_map/ppermute | solution.py:328
  24.4 11.5 %collective-permute-start.3 = (f32[2,64,128]{2,1,0:T(8,128)S(1)}, f32[2,64,128]{2,1,0:T(8,128)S(1)}, u32[]{:S(2)}, u32[]{:S(2)}) collective-permute-start(f32[2,64,128]{2,1,0:T(8,128)S(1)} %pad_maximum_fusion.refs_0_), channel_id=1, source_target_pairs={{0,48},{16,0},{32,16},{48,32},{1,49},{17,1},{33,17},{49,33},{2,50}... | collective-permute-start | bytes 196616 | tf_op jit(solution)/shard_map/ppermute | solution.py:308
  28.8 7.1 %collective-permute-start.2 = (f32[2,64,128]{2,1,0:T(8,128)S(1)}, f32[2,64,128]{2,1,0:T(8,128)S(1)}, u32[]{:S(2)}, u32[]{:S(2)}) collective-permute-start(f32[2,64,128]{2,1,0:T(8,128)S(1)} %pad_maximum_fusion.refs_0_), channel_id=1, source_target_pairs={{0,32},{16,48},{32,0},{48,16},{1,33},{17,49},{33,1},{49,17},{2,34}... | collective-permute-start | bytes 196616 | tf_op jit(solution)/shard_map/ppermute | solution.py:308
  31.2 7.6 %collective-permute-start.1 = (f32[2,64,128]{2,1,0:T(8,128)S(1)}, f32[2,64,128]{2,1,0:T(8,128)S(1)}, u32[]{:S(2)}, u32[]{:S(2)}) collective-permute-start(f32[2,64,128]{2,1,0:T(8,128)S(1)} %pad_maximum_fusion.refs_0_), channel_id=1, source_target_pairs={{0,16},{16,32},{32,48},{48,0},{1,17},{17,33},{33,49},{49,1},{2,18}... | collective-permute-start | bytes 196616 | tf_op jit(solution)/shard_map/ppermute | solution.py:308
  33.8 1.4 copy-start.1
  39.2 18.9 %collective-permute-start.4 = (f32[96,3072]{1,0:T(8,128)S(1)}, f32[96,3072]{1,0:T(8,128)S(1)}, u32[]{:S(2)}, u32[]{:S(2)}) collective-permute-start(f32[96,3072]{1,0:T(8,128)S(1)} %get-tuple-element.27.add_ref), channel_id=1, source_target_pairs={{0,1},{1,0},{2,3},{3,2},{4,5},{5,4},{6,7},{7,6},{8,9},{9,8},{10,11... | collective-permute-start | bytes 3538952 | tf_op jit(solution)/shard_map/ppermute | solution.py:346
  59.3 29.5 %all-to-all-start.2 = ((f32[32,8,384]{2,1,0:T(8,128)}), f32[32,8,384]{2,1,0:T(8,128)S(1)}, u32[]{:S(2)}, u32[]{:S(2)}) async-start(f32[32,8,384]{2,1,0:T(8,128)} %shard_map.71), calls=%async_computation.2 | async-start | bytes 786432 | tf_op jit(solution)/shard_map/all_to_all | solution.py:304
  68.1 10.6 %collective-permute-start.5 = (bf16[8,2,32,128]{3,2,1,0:T(8,128)(2,1)S(1)}, bf16[8,2,32,128]{3,2,1,0:T(8,128)(2,1)S(1)}, u32[]{:S(2)}, u32[]{:S(2)}) collective-permute-start(bf16[8,2,32,128]{3,2,1,0:T(8,128)(2,1)S(1)} %get-tuple-element.30), channel_id=1, source_target_pairs={{0,16},{16,32},{32,48},{48,0},{1,17},{17,33},{33,49},{49,1},{2,18}... | collective-permute-start | bytes 393224 | tf_op jit(solution)/shard_map/ppermute | solution.py:308
  71.2 14.8 %collective-permute-start.6 = (bf16[8,2,32,128]{3,2,1,0:T(8,128)(2,1)S(1)}, bf16[8,2,32,128]{3,2,1,0:T(8,128)(2,1)S(1)}, u32[]{:S(2)}, u32[]{:S(2)}) collective-permute-start(bf16[8,2,32,128]{3,2,1,0:T(8,128)(2,1)S(1)} %get-tuple-element.31), channel_id=1, source_target_pairs={{0,32},{16,48},{32,0},{48,16},{1,33},{17,49},{33,1},{49,17},{2,34}... | collective-permute-start | bytes 393224 | tf_op jit(solution)/shard_map/ppermute | solution.py:308
  75.6 13.1 %collective-permute-start.7 = (bf16[8,2,32,128]{3,2,1,0:T(8,128)(2,1)S(1)}, bf16[8,2,32,128]{3,2,1,0:T(8,128)(2,1)S(1)}, u32[]{:S(2)}, u32[]{:S(2)}) collective-permute-start(bf16[8,2,32,128]{3,2,1,0:T(8,128)(2,1)S(1)} %get-tuple-element.32), channel_id=1, source_target_pairs={{0,48},{16,0},{32,16},{48,32},{1,49},{17,1},{33,17},{49,33},{2,50}... | collective-permute-start | bytes 393224 | tf_op jit(solution)/shard_map/ppermute | solution.py:308
  120.0 2.8 %copy-start = (bf16[1,1024,3072]{2,1,0:T(8,128)(2,1)S(1)}, bf16[1,1024,3072]{2,1,0:T(8,128)(2,1)}, u32[]{:S(2)}) copy-start(bf16[1,1024,3072]{2,1,0:T(8,128)(2,1)} %all-gather.3.cloned.1.call-done) | copy-start | bytes 18874372
  124.5 11.9 %collective-permute-start.8 = (f32[128,3072]{1,0:T(8,128)S(1)}, f32[128,3072]{1,0:T(8,128)S(1)}, u32[]{:S(2)}, u32[]{:S(2)}) collective-permute-start(f32[128,3072]{1,0:T(8,128)S(1)} %get-tuple-element.37), channel_id=1, source_target_pairs={{0,1},{1,0},{2,3},{3,2},{4,5},{5,4},{6,7},{7,6},{8,9},{9,8},{10,11... | collective-permute-start | bytes 4718600 | tf_op jit(solution)/shard_map/ppermute | solution.py:379
  131.7 3.6 %collective-permute-start.9 = (f32[32,8,384]{2,1,0:T(8,128)S(1)}, f32[32,8,384]{2,1,0:T(8,128)S(1)}, u32[]{:S(2)}, u32[]{:S(2)}) collective-permute-start(f32[32,8,384]{2,1,0:T(8,128)S(1)} %all_to_all.32.mine_ref), channel_id=1, source_target_pairs={{0,1},{1,0},{2,3},{3,2},{4,5},{5,4},{6,7},{7,6},{8,9},{9,8},{10,11... | collective-permute-start | bytes 1179656 | tf_op jit(solution)/shard_map/ppermute | solution.py:381
  135.6 0.9 copy-start.3
  137.9 16.4 %all-to-all-start.5 = ((f32[8,64,128]{2,1,0:T(8,128)}), f32[8,64,128]{2,1,0:T(8,128)}, u32[]{:S(2)}, u32[]{:S(2)}) async-start(f32[8,64,128]{2,1,0:T(8,128)} %get-tuple-element.39), calls=%async_computation.5 | async-start | bytes 524288 | tf_op jit(solution)/shard_map/all_to_all | solution.py:304
  148.2 0.6 copy-start.7
  148.9 5.4 %copy-start.8 = (f32[64,64]{1,0:T(8,128)S(1)}, f32[64,64]{1,0:T(8,128)}, u32[]{:S(2)}) copy-start(f32[64,64]{1,0:T(8,128)} %copy-done.7) | copy-start | bytes 49156
  154.3 1.1 copy-start.4
Sparse Core Ops, SparseCore 0:
  11.2 106.5 all-gather.2

commit v4 on v3

--- a/solution.py
+++ b/solution.py
@@ -355,17 +355,22 @@
     )
     late_cut = after(cut, left)
     chip = shaped(deep, 2, count, own, dtype=BF16)
-    columns = vmem_call(pick_columns, (chip,) * across, late_cut)
-    columns = [columns[0]] + [shifted(columns[s], across, s) for s in range(1, across)]
+    columns = list(vmem_call(pick_columns, (chip,) * across, late_cut))
+    far = across // 2
+    near = [s for s in range(1, across) if s != far]
+    for s in near:
+        columns[s] = shifted(columns[s], across, s)
+    left = direct(left, PEERS)
+    left = after(left, [columns[s] for s in near])
+    left = vmem_call(add_spread, shaped(deep, 8, width), left)
+    columns[far] = shifted(after(columns[far], left), across, far)
+    left = direct(left, "z")
+    summed = vmem_call(add_spread, shaped(peers, 8, width), after(left, columns[far]))
     columns = vmem_call(
         turn_columns,
         shaped(2 * own, deep * across * count, dtype=BF16),
         *columns,
     )
-    left = direct(left, PEERS)
-    left = vmem_call(add_spread, shaped(deep, 8, width), after(left, columns))
-    left = direct(left, "z")
-    summed = vmem_call(add_spread, shaped(peers, 8, width), left)
     left = direct(summed, PEERS)
     gathered = after(gathered, left)
     grad_keep, grad_send = vmem_call(

time: 167 us -> 164 us (0.982)
  blocking collectives: 47.2 us -> 16.3 us
  waiting for transfers between devices: 21 us -> 37.8 us
  starting transfers between devices: 58.2 us -> 69.3 us
    all_to_all x3 -> x1, blocking collectives: 47.2 us -> 16.3 us  [direct(): return lax.all_to_all(blocks, axes, split_axis=0, concat_axis=0, tiled=True)]
    all_to_all x3 -> x5, waiting for transfers between devices: 4.96 us -> 17.1 us  [direct(): return lax.all_to_all(blocks, axes, split_axis=0, concat_axis=0, tiled=True)]
    all_to_all x3 -> x5, starting transfers between devices: 23.6 us -> 34.9 us  [direct(): return lax.all_to_all(blocks, axes, split_axis=0, concat_axis=0, tiled=True)]
    ppermute x6, waiting for transfers between devices: 12.8 us -> 17.5 us  [shifted(): lax.ppermute(value, 'x', [(i, (i + shift) % across) for i in range(across)])]
    unnamed x18 -> x20, local copies, waits for them, and re-layouts: 7.86 us -> 7.95 us
  transfers between devices with their start and end apart: 14 -> 16, of which waited for: 6 -> 8; matrix products, arithmetic and copies ran while one was open for 0% -> 0% of each run, Pallas kernels for 6% -> 7%
where the time goes in v4:
time: 164 us; the launch traced here: 163 us
  starting transfers between devices  69.3 us (42%)
  waiting for transfers between devices  37.8 us (23%)
  Pallas kernels  17.2 us (10%)
  blocking collectives  16.3 us (10%)
  between operations  14.3 us (9%)
  local copies, waits for them, and re-layouts  7.95 us (5%)
    all_to_all x5, starting transfers between devices, direct(): return lax.all_to_all(blocks, axes, split_axis=0, concat_axis=0, tiled=True)  34.9 us
    ppermute x6, starting transfers between devices, shifted(): lax.ppermute(value, 'x', [(i, (i + shift) % across) for i in range(across)])  20.5 us
    ppermute x6, waiting for transfers between devices, shifted(): lax.ppermute(value, 'x', [(i, (i + shift) % across) for i in range(across)])  17.5 us
    all_to_all x5, waiting for transfers between devices, direct(): return lax.all_to_all(blocks, axes, split_axis=0, concat_axis=0, tiled=True)  17.1 us
    all_to_all x1, blocking collectives, direct(): return lax.all_to_all(blocks, axes, split_axis=0, concat_axis=0, tiled=True)  16.3 us
    pallas_call x14, Pallas kernels, vmem_call(): pl.pallas_call(body, out_shape=out_shape, in_specs=[whole] * len(args), o...  14.4 us
    unnamed x20, local copies, waits for them, and re-layouts  7.95 us
    ppermute x1, starting transfers between devices, per_device(): grad_in = lax.ppermute(grad_send, 'core', SWAP)  6.3 us
  transfers between devices with their start and end apart: 16, of which 8 were waited for; matrix products, arithmetic and copies ran while one was open for 0% of the time, Pallas kernels for 7%

profile of v4, /device:TPU:1, one launch (start us, length us, event | category | flops | bytes accessed | tf_op | source)
XLA Modules:
  0.0 162.8 jit_solution(17220505692369688548)
XLA Ops:
  9.8 10.9 %all-to-all-start = ((bf16[8,8,32,128]{3,2,1,0:T(8,128)(2,1)}), bf16[8,8,32,128]{3,2,1,0:T(8,128)(2,1)S(1)}, u32[]{:S(2)}, u32[]{:S(2)}) async-start(bf16[8,8,32,128]{3,2,1,0:T(8,128)(2,1)} %shard_map.67), calls=%async_computation | async-start | bytes 1048576 | tf_op jit(solution)/shard_map/all_to_all | solution.py:304
  20.7 2.9 %collective-permute-start = (f32[64,128]{1,0:T(8,128)S(1)}, f32[64,128]{1,0:T(8,128)S(1)}, u32[]{:S(2)}, u32[]{:S(2)}) collective-permute-start(f32[64,128]{1,0:T(8,128)S(1)} %bitcast.13), channel_id=1, source_target_pairs={{0,1},{1,0},{2,3},{3,2},{4,5},{5,4},{6,7},{7,6},{8,9},{9,8},{10,11... | collective-permute-start | bytes 98312 | tf_op jit(solution)/shard_map/ppermute | solution.py:328
  24.4 4.4 %collective-permute-start.3 = (f32[2,64,128]{2,1,0:T(8,128)S(1)}, f32[2,64,128]{2,1,0:T(8,128)S(1)}, u32[]{:S(2)}, u32[]{:S(2)}) collective-permute-start(f32[2,64,128]{2,1,0:T(8,128)S(1)} %pad_maximum_fusion.refs_0_), channel_id=1, source_target_pairs={{0,48},{16,0},{32,16},{48,32},{1,49},{17,1},{33,17},{49,33},{2,50}... | collective-permute-start | bytes 196616 | tf_op jit(solution)/shard_map/ppermute | solution.py:308
  28.8 2.4 %collective-permute-start.2 = (f32[2,64,128]{2,1,0:T(8,128)S(1)}, f32[2,64,128]{2,1,0:T(8,128)S(1)}, u32[]{:S(2)}, u32[]{:S(2)}) collective-permute-start(f32[2,64,128]{2,1,0:T(8,128)S(1)} %pad_maximum_fusion.refs_0_), channel_id=1, source_target_pairs={{0,32},{16,48},{32,0},{48,16},{1,33},{17,49},{33,1},{49,17},{2,34}... | collective-permute-start | bytes 196616 | tf_op jit(solution)/shard_map/ppermute | solution.py:308
  31.2 2.5 %collective-permute-start.1 = (f32[2,64,128]{2,1,0:T(8,128)S(1)}, f32[2,64,128]{2,1,0:T(8,128)S(1)}, u32[]{:S(2)}, u32[]{:S(2)}) collective-permute-start(f32[2,64,128]{2,1,0:T(8,128)S(1)} %pad_maximum_fusion.refs_0_), channel_id=1, source_target_pairs={{0,16},{16,32},{32,48},{48,0},{1,17},{17,33},{33,49},{49,1},{2,18}... | collective-permute-start | bytes 196616 | tf_op jit(solution)/shard_map/ppermute | solution.py:308
  36.0 2.8 %collective-permute-done.1.refs_1_ = f32[2,64,128]{2,1,0:T(8,128)S(1)} collective-permute-done((f32[2,64,128]{2,1,0:T(8,128)S(1)}, f32[2,64,128]{2,1,0:T(8,128)S(1)}, u32[]{:S(2)}, u32[]{:S(2)}) %collective-permute-start.1) | collective-permute-done | bytes 65568 | tf_op jit(solution)/shard_map/ppermute | solution.py:308
  39.2 2.8 %collective-permute-start.4 = (f32[96,3072]{1,0:T(8,128)}, f32[96,3072]{1,0:T(8,128)S(1)}, u32[]{:S(2)}, u32[]{:S(2)}) collective-permute-start(f32[96,3072]{1,0:T(8,128)} %copy-done.2), channel_id=1, source_target_pairs={{0,1},{1,0},{2,3},{3,2},{4,5},{5,4},{6,7},{7,6},{8,9},{9,8},{10,11... | collective-permute-start | bytes 3538952 | tf_op jit(solution)/shard_map/ppermute | solution.py:346
  42.0 16.3 %all_to_all.30.y_ref = f32[16,16,128]{2,1,0:T(8,128)S(1)} all-to-all(f32[16,16,128]{2,1,0:T(8,128)S(1)} %shard_map.69), channel_id=1, replica_groups=mesh['rep'=8,'x'=4,'z'=8,'core'=2] {'z','core'}, dimensions={0} | all-to-all | bytes 262144 | tf_op jit(solution)/shard_map/all_to_all | solution.py:304
  59.5 8.6 %all-to-all-start.2 = ((f32[32,8,384]{2,1,0:T(8,128)}), f32[32,8,384]{2,1,0:T(8,128)S(1)}, u32[]{:S(2)}, u32[]{:S(2)}) async-start(f32[32,8,384]{2,1,0:T(8,128)} %shard_map.71), calls=%async_computation.2 | async-start | bytes 786432 | tf_op jit(solution)/shard_map/all_to_all | solution.py:304
  68.1 3.1 %collective-permute-start.5 = (bf16[8,2,32,128]{3,2,1,0:T(8,128)(2,1)S(1)}, bf16[8,2,32,128]{3,2,1,0:T(8,128)(2,1)S(1)}, u32[]{:S(2)}, u32[]{:S(2)}) collective-permute-start(bf16[8,2,32,128]{3,2,1,0:T(8,128)(2,1)S(1)} %get-tuple-element.32), channel_id=1, source_target_pairs={{0,16},{16,32},{32,48},{48,0},{1,17},{17,33},{33,49},{49,1},{2,18}... | collective-permute-start | bytes 393224 | tf_op jit(solution)/shard_map/ppermute | solution.py:308
  71.3 3.4 %collective-permute-start.6 = (bf16[8,2,32,128]{3,2,1,0:T(8,128)(2,1)S(1)}, bf16[8,2,32,128]{3,2,1,0:T(8,128)(2,1)S(1)}, u32[]{:S(2)}, u32[]{:S(2)}) collective-permute-start(bf16[8,2,32,128]{3,2,1,0:T(8,128)(2,1)S(1)} %get-tuple-element.34), channel_id=1, source_target_pairs={{0,48},{16,0},{32,16},{48,32},{1,49},{17,1},{33,17},{49,33},{2,50}... | collective-permute-start | bytes 393224 | tf_op jit(solution)/shard_map/ppermute | solution.py:308
  74.6 2.0 %collective-permute-done.5.refs_1_ = bf16[8,2,32,128]{3,2,1,0:T(8,128)(2,1)S(1)} collective-permute-done((bf16[8,2,32,128]{3,2,1,0:T(8,128)(2,1)S(1)}, bf16[8,2,32,128]{3,2,1,0:T(8,128)(2,1)S(1)}, u32[]{:S(2)}, u32[]{:S(2)}) %collective-permute-start.5) | collective-permute-done | bytes 131104 | tf_op jit(solution)/shard_map/ppermute | solution.py:308
  76.6 6.3 %collective-permute-done.6.refs_3_ = bf16[8,2,32,128]{3,2,1,0:T(8,128)(2,1)S(1)} collective-permute-done((bf16[8,2,32,128]{3,2,1,0:T(8,128)(2,1)S(1)}, bf16[8,2,32,128]{3,2,1,0:T(8,128)(2,1)S(1)}, u32[]{:S(2)}, u32[]{:S(2)}) %collective-permute-start.6) | collective-permute-done | bytes 131104 | tf_op jit(solution)/shard_map/ppermute | solution.py:308
  83.6 3.4 %all-to-all-start.3 = ((f32[8,8,384]{2,1,0:T(8,128)}), f32[8,8,384]{2,1,0:T(8,128)S(1)}, u32[]{:S(2)}, u32[]{:S(2)}) async-start(f32[8,8,384]{2,1,0:T(8,128)} %shard_map.73), calls=%async_computation.3 | async-start | bytes 196608 | tf_op jit(solution)/shard_map/all_to_all | solution.py:304
  87.0 4.7 %collective-permute-start.7 = (bf16[8,2,32,128]{3,2,1,0:T(8,128)(2,1)S(1)}, bf16[8,2,32,128]{3,2,1,0:T(8,128)(2,1)S(1)}, u32[]{:S(2)}, u32[]{:S(2)}) collective-permute-start(bf16[8,2,32,128]{3,2,1,0:T(8,128)(2,1)S(1)} %get-tuple-element.36), channel_id=1, source_target_pairs={{0,32},{16,48},{32,0},{48,16},{1,33},{17,49},{33,1},{49,17},{2,34}... | collective-permute-start | bytes 393224 | tf_op jit(solution)/shard_map/ppermute | solution.py:308
  91.7 6.4 %collective-permute-done.7.refs_2_ = bf16[8,2,32,128]{3,2,1,0:T(8,128)(2,1)S(1)} collective-permute-done((bf16[8,2,32,128]{3,2,1,0:T(8,128)(2,1)S(1)}, bf16[8,2,32,128]{3,2,1,0:T(8,128)(2,1)S(1)}, u32[]{:S(2)}, u32[]{:S(2)}) %collective-permute-start.7) | collective-permute-done | bytes 131104 | tf_op jit(solution)/shard_map/ppermute | solution.py:308
  98.8 8.7 %all-to-all-start.4 = ((f32[32,8,384]{2,1,0:T(8,128)}), f32[32,8,384]{2,1,0:T(8,128)S(1)}, u32[]{:S(2)}, u32[]{:S(2)}) async-start(f32[32,8,384]{2,1,0:T(8,128)} %shard_map.75), calls=%async_computation.4 | async-start | bytes 786432 | tf_op jit(solution)/shard_map/all_to_all | solution.py:304
  107.7 11.6 %all-to-all-done.4.mine_ref = f32[32,8,384]{2,1,0:T(8,128)S(1)} async-done(((f32[32,8,384]{2,1,0:T(8,128)}), f32[32,8,384]{2,1,0:T(8,128)S(1)}, u32[]{:S(2)}, u32[]{:S(2)}) %all-to-all-start.4) | async-done | bytes 393248 | tf_op jit(solution)/shard_map/all_to_all | solution.py:304
  119.3 2.8 %copy-done = bf16[1,1024,3072]{2,1,0:T(8,128)(2,1)S(1)} copy-done((bf16[1,1024,3072]{2,1,0:T(8,128)(2,1)S(1)}, bf16[1,1024,3072]{2,1,0:T(8,128)(2,1)}, u32[]{:S(2)}) %copy-start) | copy-done | bytes 6291480
  123.9 6.3 %collective-permute-start.8 = (f32[128,3072]{1,0:T(8,128)S(1)}, f32[128,3072]{1,0:T(8,128)S(1)}, u32[]{:S(2)}, u32[]{:S(2)}) collective-permute-start(f32[128,3072]{1,0:T(8,128)S(1)} %get-tuple-element.41), channel_id=1, source_target_pairs={{0,1},{1,0},{2,3},{3,2},{4,5},{5,4},{6,7},{7,6},{8,9},{9,8},{10,11... | collective-permute-start | bytes 4718600 | tf_op jit(solution)/shard_map/ppermute | solution.py:384
  136.4 3.4 %all-to-all-start.5 = ((f32[8,64,128]{2,1,0:T(8,128)}), f32[8,64,128]{2,1,0:T(8,128)S(1)}, u32[]{:S(2)}, u32[]{:S(2)}) async-start(f32[8,64,128]{2,1,0:T(8,128)} %copy-done.8), calls=%async_computation.5 | async-start | bytes 524288 | tf_op jit(solution)/shard_map/all_to_all | solution.py:304
  139.8 6.3 %shard_map.79.inverse_ref = f32[64,64]{1,0:T(8,128)S(1)} custom-call(f32[32,8,384]{2,1,0:T(8,128)S(1)} %all-to-all-done.4.mine_ref, f32[32,8,384]{2,1,0:T(8,128)S(1)} %collective-permute-done.9.other_ref), custom_call_target="tpu_custom_call" | custom-call | flops 150994944 | bytes 802816 | tf_op jit(solution)/shard_map/pallas_call | solution.py:53
  146.6 5.5 %all-to-all-done.5.right_ref = f32[8,64,128]{2,1,0:T(8,128)S(1)} async-done(((f32[8,64,128]{2,1,0:T(8,128)}), f32[8,64,128]{2,1,0:T(8,128)S(1)}, u32[]{:S(2)}, u32[]{:S(2)}) %all-to-all-start.5) | async-done | bytes 262176 | tf_op jit(solution)/shard_map/all_to_all | solution.py:304
  153.2 2.8 %shard_map.81 = (bf16[3072,128]{1,0:T(8,128)(2,1)}, f32[3072,128]{1,0:T(8,128)}, f32[64,128]{1,0:T(8,128)}) custom-call(f32[8,64,128]{2,1,0:T(8,128)S(1)} %all-to-all-done.5.right_ref, f32[64,64]{1,0:T(8,128)S(1)} %shard_map.79.inverse_ref, bf16[3072,128]{1,0:T(8,128)(2,1)S(1)} %copy-done.6, f32[3072,128]{1,0:T(8,128)S(1)} %shard_map.80.merged_ref), custom_call_target="tpu_custom_call" | custom-call | flops 150994944 | bytes 5013504 | tf_op jit(solution)/shard_map/pallas_call | solution.py:282
  (46 shorter events, 18.5 us)
Async XLA Ops:
  7.2 26.6 %copy-start.4 = (bf16[1,32,3072]{2,1,0:T(8,128)(2,1)S(1)}, bf16[1,32,3072]{2,1,0:T(8,128)(2,1)}, u32[]{:S(2)}) copy-start(bf16[1,32,3072]{2,1,0:T(8,128)(2,1)} %param.4) | copy-start | bytes 589828
  7.2 112.1 %all-gather.3.cloned.1.call-start = ((), (), s32[]{:S(2)}) async-start(), calls=%async_computation.6 | async-start | bytes 6488064 | tf_op jit(solution)/shard_map/all_gather | solution.py:323
  7.9 1.0 copy-start.7
  9.0 11.8 %copy-start.9 = (f32[128,64]{0,1:T(8,128)S(1)}, f32[128,64]{0,1:T(8,128)}, u32[]{:S(2)}) copy-start(f32[128,64]{0,1:T(8,128)} %param.7) | copy-start | bytes 98308
  9.8 29.0 %all-to-all-start = ((bf16[8,8,32,128]{3,2,1,0:T(8,128)(2,1)}), bf16[8,8,32,128]{3,2,1,0:T(8,128)(2,1)S(1)}, u32[]{:S(2)}, u32[]{:S(2)}) async-start(bf16[8,8,32,128]{3,2,1,0:T(8,128)(2,1)} %shard_map.67), calls=%async_computation | async-start | bytes 1048576 | tf_op jit(solution)/shard_map/all_to_all | solution.py:304
  20.7 3.7 %collective-permute-start = (f32[64,128]{1,0:T(8,128)S(1)}, f32[64,128]{1,0:T(8,128)S(1)}, u32[]{:S(2)}, u32[]{:S(2)}) collective-permute-start(f32[64,128]{1,0:T(8,128)S(1)} %bitcast.13), channel_id=1, source_target_pairs={{0,1},{1,0},{2,3},{3,2},{4,5},{5,4},{6,7},{7,6},{8,9},{9,8},{10,11... | collective-permute-start | bytes 98312 | tf_op jit(solution)/shard_map/ppermute | solution.py:328
  24.4 11.5 %collective-permute-start.3 = (f32[2,64,128]{2,1,0:T(8,128)S(1)}, f32[2,64,128]{2,1,0:T(8,128)S(1)}, u32[]{:S(2)}, u32[]{:S(2)}) collective-permute-start(f32[2,64,128]{2,1,0:T(8,128)S(1)} %pad_maximum_fusion.refs_0_), channel_id=1, source_target_pairs={{0,48},{16,0},{32,16},{48,32},{1,49},{17,1},{33,17},{49,33},{2,50}... | collective-permute-start | bytes 196616 | tf_op jit(solution)/shard_map/ppermute | solution.py:308
  28.8 7.2 %collective-permute-start.2 = (f32[2,64,128]{2,1,0:T(8,128)S(1)}, f32[2,64,128]{2,1,0:T(8,128)S(1)}, u32[]{:S(2)}, u32[]{:S(2)}) collective-permute-start(f32[2,64,128]{2,1,0:T(8,128)S(1)} %pad_maximum_fusion.refs_0_), channel_id=1, source_target_pairs={{0,32},{16,48},{32,0},{48,16},{1,33},{17,49},{33,1},{49,17},{2,34}... | collective-permute-start | bytes 196616 | tf_op jit(solution)/shard_map/ppermute | solution.py:308
  31.2 7.6 %collective-permute-start.1 = (f32[2,64,128]{2,1,0:T(8,128)S(1)}, f32[2,64,128]{2,1,0:T(8,128)S(1)}, u32[]{:S(2)}, u32[]{:S(2)}) collective-permute-start(f32[2,64,128]{2,1,0:T(8,128)S(1)} %pad_maximum_fusion.refs_0_), channel_id=1, source_target_pairs={{0,16},{16,32},{32,48},{48,0},{1,17},{17,33},{33,49},{49,1},{2,18}... | collective-permute-start | bytes 196616 | tf_op jit(solution)/shard_map/ppermute | solution.py:308
  33.8 1.4 copy-start.1
  35.9 2.9 %copy-start.2 = (f32[96,3072]{1,0:T(8,128)}, f32[96,3072]{1,0:T(8,128)S(1)}, u32[]{:S(2)}) copy-start(f32[96,3072]{1,0:T(8,128)S(1)} %get-tuple-element.29.add_ref) | copy-start | bytes 3538948
  38.9 19.5 %copy-start.3 = (f32[96,3072]{1,0:T(8,128)S(1)}, f32[96,3072]{1,0:T(8,128)}, u32[]{:S(2)}) copy-start(f32[96,3072]{1,0:T(8,128)} %copy-done.2) | copy-start | bytes 3538948
  39.2 19.1 %collective-permute-start.4 = (f32[96,3072]{1,0:T(8,128)}, f32[96,3072]{1,0:T(8,128)S(1)}, u32[]{:S(2)}, u32[]{:S(2)}) collective-permute-start(f32[96,3072]{1,0:T(8,128)} %copy-done.2), channel_id=1, source_target_pairs={{0,1},{1,0},{2,3},{3,2},{4,5},{5,4},{6,7},{7,6},{8,9},{9,8},{10,11... | collective-permute-start | bytes 3538952 | tf_op jit(solution)/shard_map/ppermute | solution.py:346
  59.5 23.5 %all-to-all-start.2 = ((f32[32,8,384]{2,1,0:T(8,128)}), f32[32,8,384]{2,1,0:T(8,128)S(1)}, u32[]{:S(2)}, u32[]{:S(2)}) async-start(f32[32,8,384]{2,1,0:T(8,128)} %shard_map.71), calls=%async_computation.2 | async-start | bytes 786432 | tf_op jit(solution)/shard_map/all_to_all | solution.py:304
  68.1 8.5 %collective-permute-start.5 = (bf16[8,2,32,128]{3,2,1,0:T(8,128)(2,1)S(1)}, bf16[8,2,32,128]{3,2,1,0:T(8,128)(2,1)S(1)}, u32[]{:S(2)}, u32[]{:S(2)}) collective-permute-start(bf16[8,2,32,128]{3,2,1,0:T(8,128)(2,1)S(1)} %get-tuple-element.32), channel_id=1, source_target_pairs={{0,16},{16,32},{32,48},{48,0},{1,17},{17,33},{33,49},{49,1},{2,18}... | collective-permute-start | bytes 393224 | tf_op jit(solution)/shard_map/ppermute | solution.py:308
  71.3 11.7 %collective-permute-start.6 = (bf16[8,2,32,128]{3,2,1,0:T(8,128)(2,1)S(1)}, bf16[8,2,32,128]{3,2,1,0:T(8,128)(2,1)S(1)}, u32[]{:S(2)}, u32[]{:S(2)}) collective-permute-start(bf16[8,2,32,128]{3,2,1,0:T(8,128)(2,1)S(1)} %get-tuple-element.34), channel_id=1, source_target_pairs={{0,48},{16,0},{32,16},{48,32},{1,49},{17,1},{33,17},{49,33},{2,50}... | collective-permute-start | bytes 393224 | tf_op jit(solution)/shard_map/ppermute | solution.py:308
  83.6 14.4 %all-to-all-start.3 = ((f32[8,8,384]{2,1,0:T(8,128)}), f32[8,8,384]{2,1,0:T(8,128)S(1)}, u32[]{:S(2)}, u32[]{:S(2)}) async-start(f32[8,8,384]{2,1,0:T(8,128)} %shard_map.73), calls=%async_computation.3 | async-start | bytes 196608 | tf_op jit(solution)/shard_map/all_to_all | solution.py:304
  87.0 11.0 %collective-permute-start.7 = (bf16[8,2,32,128]{3,2,1,0:T(8,128)(2,1)S(1)}, bf16[8,2,32,128]{3,2,1,0:T(8,128)(2,1)S(1)}, u32[]{:S(2)}, u32[]{:S(2)}) collective-permute-start(bf16[8,2,32,128]{3,2,1,0:T(8,128)(2,1)S(1)} %get-tuple-element.36), channel_id=1, source_target_pairs={{0,32},{16,48},{32,0},{48,16},{1,33},{17,49},{33,1},{49,17},{2,34}... | collective-permute-start | bytes 393224 | tf_op jit(solution)/shard_map/ppermute | solution.py:308
  98.8 20.5 %all-to-all-start.4 = ((f32[32,8,384]{2,1,0:T(8,128)}), f32[32,8,384]{2,1,0:T(8,128)S(1)}, u32[]{:S(2)}, u32[]{:S(2)}) async-start(f32[32,8,384]{2,1,0:T(8,128)} %shard_map.75), calls=%async_computation.4 | async-start | bytes 786432 | tf_op jit(solution)/shard_map/all_to_all | solution.py:304
  119.3 2.8 %copy-start = (bf16[1,1024,3072]{2,1,0:T(8,128)(2,1)S(1)}, bf16[1,1024,3072]{2,1,0:T(8,128)(2,1)}, u32[]{:S(2)}) copy-start(bf16[1,1024,3072]{2,1,0:T(8,128)(2,1)} %all-gather.3.cloned.1.call-done) | copy-start | bytes 18874372
  123.9 11.1 %collective-permute-start.8 = (f32[128,3072]{1,0:T(8,128)S(1)}, f32[128,3072]{1,0:T(8,128)S(1)}, u32[]{:S(2)}, u32[]{:S(2)}) collective-permute-start(f32[128,3072]{1,0:T(8,128)S(1)} %get-tuple-element.41), channel_id=1, source_target_pairs={{0,1},{1,0},{2,3},{3,2},{4,5},{5,4},{6,7},{7,6},{8,9},{9,8},{10,11... | collective-permute-start | bytes 4718600 | tf_op jit(solution)/shard_map/ppermute | solution.py:384
  130.2 3.6 %collective-permute-start.9 = (f32[32,8,384]{2,1,0:T(8,128)S(1)}, f32[32,8,384]{2,1,0:T(8,128)S(1)}, u32[]{:S(2)}, u32[]{:S(2)}) collective-permute-start(f32[32,8,384]{2,1,0:T(8,128)S(1)} %all-to-all-done.4.mine_ref), channel_id=1, source_target_pairs={{0,1},{1,0},{2,3},{3,2},{4,5},{5,4},{6,7},{7,6},{8,9},{9,8},{10,11... | collective-permute-start | bytes 1179656 | tf_op jit(solution)/shard_map/ppermute | solution.py:386
  136.4 15.7 %all-to-all-start.5 = ((f32[8,64,128]{2,1,0:T(8,128)}), f32[8,64,128]{2,1,0:T(8,128)S(1)}, u32[]{:S(2)}, u32[]{:S(2)}) async-start(f32[8,64,128]{2,1,0:T(8,128)} %copy-done.8), calls=%async_computation.5 | async-start | bytes 524288 | tf_op jit(solution)/shard_map/all_to_all | solution.py:304
  152.1 1.1 copy-start.6
  (2 other events, 1.6 us)
Sparse Core Ops, SparseCore 0:
  11.2 104.1 all-gather.2
